TPU v7x, 512 devices: a whole 4x8x8 slice. The times are simulated.
512 devices in a mesh: gx: 8 (over x, core), gy: 8 (over z), gz: 8 (over y).
Axes of the slice: x: 4, y: 8, z: 8, core: 2. Of those that a mesh axis runs over, the one named last changes fastest.
Arguments:
- prior_basis: float32 [32, 128, 12288], P('gx', 'gy', 'gz'), may hold values from -6 to 6
- edge_weights: float32 [3, 32, 128, 128], P(None, 'gx', 'gy', 'gz'), may hold values from 0.5 to 1.5
- spectral_shift: float32 [1], replicated, may hold values from 0.5 to 4
Outputs:
- new_basis: float32 [32, 128, 16384], P('gx', 'gy', 'gz')
- projection: float32 [96, 128], replicated
- triangle: float32 [128, 128], replicated
All inputs are finite; a program needn't handle non-finite values.
Results may differ from a plain program's by a relative error of at most 0.002.
Values sent between devices are 32-bit elements; how exact they have to be, the bound alone decides.
A program may use at most 64 MiB of HBM per device.

v0:
```python
import jax
import jax.numpy as jnp
from jax import lax
from jax.sharding import PartitionSpec as P

BLOCK = 32
POWERS = 4
BASIS = 96


PRECISE = lax.Precision.HIGHEST
OPERATOR_SCALE = 11.0


def passed_along(block, axis, distance):
    devices = range(lax.axis_size(axis))
    route = [(i - distance, i) for i in devices if i - distance in devices]
    return lax.ppermute(block, axis, route)


def with_halo(block, sides, width):
    for axis, dim in sides:
        count = lax.axis_size(axis)
        forward = [(i, i + 1) for i in range(count - 1)]
        backward = [(target, source) for source, target in forward]
        low = lax.ppermute(
            lax.slice_in_dim(block, block.shape[dim] - width, None, axis=dim), axis, forward
        )
        high = lax.ppermute(lax.slice_in_dim(block, 0, width, axis=dim), axis, backward)
        block = jnp.concatenate([low, block, high], axis=dim)
    return block


def crop_margin(values, layers, columns):
    return values[
        ...,
        layers : values.shape[-3] - layers,
        layers : values.shape[-2] - layers,
        layers * columns : values.shape[-1] - layers * columns,
    ]


def stencil(padded, weight_pad, shift_value, columns):
    centre = crop_margin(padded, 1, columns)
    inner_weights = crop_margin(weight_pad, 1, columns)
    below_x = weight_pad[0, :-2, 1:-1, columns:-columns]
    below_y = weight_pad[1, 1:-1, :-2, columns:-columns]
    below_z = weight_pad[2, 1:-1, 1:-1, : -2 * columns]
    summed = inner_weights[0] * (centre - padded[2:, 1:-1, columns:-columns]) + below_x * (
        centre - padded[:-2, 1:-1, columns:-columns]
    )
    summed = (
        summed
        + inner_weights[1] * (centre - padded[1:-1, 2:, columns:-columns])
        + below_y * (centre - padded[1:-1, :-2, columns:-columns])
    )
    summed = (
        summed
        + inner_weights[2] * (centre - padded[1:-1, 1:-1, 2 * columns :])
        + below_z * (centre - padded[1:-1, 1:-1, : -2 * columns])
    )
    return (summed + shift_value * centre) / OPERATOR_SCALE - centre


def per_device(prior_basis, edge_weights, spectral_shift):
    size_x = prior_basis.shape[0]
    size_y = prior_basis.shape[1]
    size_z = prior_basis.shape[2] // BASIS
    cell_local = size_x * size_y * size_z
    cell_count = cell_local * lax.axis_size("gx") * lax.axis_size("gy") * lax.axis_size("gz")
    shift_value = spectral_shift[0]
    basis_rows = prior_basis.reshape(cell_local, BASIS)
    start_block = prior_basis.reshape(size_x, size_y, size_z, BASIS)[..., BASIS - BLOCK :]
    lower_x = passed_along(edge_weights[0, size_x - 1 :], "gx", 1)
    lower_y = passed_along(edge_weights[1, :, size_y - 1 :], "gy", 1)
    lower_z = passed_along(edge_weights[2, :, :, size_z - 1 :], "gz", 1)
    weight_pad = jnp.pad(edge_weights, ((0, 0), (1, 1), (1, 1), (1, 1)))
    weight_pad = weight_pad.at[0, 0:1, 1:-1, 1:-1].set(lower_x)
    weight_pad = weight_pad.at[1, 1:-1, 0:1, 1:-1].set(lower_y)
    weight_pad = weight_pad.at[2, 1:-1, 1:-1, 0:1].set(lower_z)
    weight_pad = jnp.repeat(weight_pad, BLOCK, axis=3)

    def apply_once(field):
        padded = with_halo(field, (("gx", 0), ("gy", 1), ("gz", 2)), 1)
        padded = padded.reshape(size_x + 2, size_y + 2, (size_z + 2) * BLOCK)
        return stencil(padded, weight_pad, shift_value, BLOCK).reshape(
            size_x, size_y, size_z, BLOCK
        )

    previous = start_block
    current = apply_once(start_block)
    powers = [current]
    for degree in range(1, POWERS):
        following = 2.0 * apply_once(current) - previous
        previous, current = (current, following)
        powers.append(following)
    krylov = jnp.stack(powers, axis=3).reshape(cell_local, BLOCK * POWERS)
    first_coef = (
        lax.psum(jnp.dot(basis_rows.T, krylov, precision=PRECISE), ("gx", "gy", "gz")) / cell_count
    )
    once = krylov - jnp.dot(basis_rows, first_coef, precision=PRECISE)
    second_coef = (
        lax.psum(jnp.dot(basis_rows.T, once, precision=PRECISE), ("gx", "gy", "gz")) / cell_count
    )
    twice = once - jnp.dot(basis_rows, second_coef, precision=PRECISE)
    gram_matrix = (
        lax.psum(jnp.dot(twice.T, twice, precision=PRECISE), ("gx", "gy", "gz")) / cell_count
    )
    lower_factor = jnp.linalg.cholesky(gram_matrix)
    solved = jax.scipy.linalg.solve_triangular(lower_factor, twice.T, lower=True)
    new_basis = solved.T.reshape(size_x, size_y, size_z * BLOCK * POWERS)
    return (new_basis, first_coef + second_coef, lower_factor.T)


def solution(mesh):
    return jax.shard_map(
        per_device,
        mesh=mesh,
        in_specs=(P("gx", "gy", "gz"), P(None, "gx", "gy", "gz"), P()),
        out_specs=(P("gx", "gy", "gz"), P(), P()),
        check_vma=False,
    )
```

profile of v0, /device:TPU:1, one launch (start us, length us, event | category | flops | bytes accessed | tf_op | source)
XLA Modules:
  0.0 644.6 jit_solution(5951552109017409170)
XLA Ops:
  8.5 4.5 collective-permute-start.3
  13.1 5.6 collective-permute-start.4
  19.6 3.7 collective-permute-start.5
  28.9 3.2 collective-permute-start.7
  33.6 4.0 collective-permute-start.2
  37.6 4.0 collective-permute-start.1
  44.4 2.5 broadcast_in_dim.5
  46.9 3.1 reshape.205
  52.9 4.1 collective-permute-start.9
  59.3 4.3 collective-permute-done.10
  63.6 5.2 collective-permute-start.11
  70.1 5.1 collective-permute-done.12
  75.4 3.2 collective-permute-start.13
  79.9 4.2 collective-permute-done.14
  85.6 4.5 collective-permute-start.15
  92.1 4.3 collective-permute-done.16
  96.4 3.4 collective-permute-start.17
  101.2 3.6 collective-permute-done.18
  104.9 4.9 collective-permute-start.19
  111.1 3.9 collective-permute-done.20
  117.0 4.8 collective-permute-start.21
  123.9 4.3 collective-permute-done.22
  128.2 4.8 collective-permute-start.23
  134.3 4.1 collective-permute-done.24
  139.2 4.3 collective-permute-start.25
  154.9 2.7 copy.16
  157.6 2.4 reshape.212
  161.2 95.3 %psum.21 = f32[96,128]{1,0:T(8,128)S(1)} all-reduce(f32[96,128]{1,0:T(8,128)S(1)} %convolution_bitcast_fusion.3), channel_id=1, replica_groups=mesh['gx'=8,'gy'=8,'gz'=8] {'gx','gy','gz'}, use_global_device_ids=true, to_apply=%region_0.1 | all-reduce | flops 12288 | bytes 98304 | tf_op jit(solution)/shard_map/psum | solution.py:99
  258.2 94.9 %psum.22 = f32[96,128]{1,0:T(8,128)S(1)} all-reduce(f32[96,128]{1,0:T(8,128)S(1)} %convolution_bitcast_fusion.2), channel_id=1, replica_groups=mesh['gx'=8,'gy'=8,'gz'=8] {'gx','gy','gz'}, use_global_device_ids=true, to_apply=%region_1.2 | all-reduce | flops 12288 | bytes 98304 | tf_op jit(solution)/shard_map/psum | solution.py:103
  355.6 254.9 %all-reduce.3.cloned.1.call-done = f32[128,128]{0,1:T(8,128)} async-done(((f32[128,128]{0,1:T(8,128)}), f32[128,128]{0,1:T(8,128)}) %all-reduce.3.cloned.1.call-update) | async-done | bytes 65552 | tf_op jit(solution)/shard_map/psum | solution.py:107
  612.3 11.7 %cholesky.16 = f32[128,128]{1,0:T(8,128)S(1)} custom-call(f32[128,128]{1,0:T(8,128)S(1)} %fusion.63), custom_call_target="Cholesky" | custom-call | tf_op jit(solution)/shard_map/jit(cholesky)/cholesky | solution.py:109
  625.4 9.8 %custom-call.7 = f32[1,128,128]{1,2,0:T(8,128)S(1)} custom-call(f32[1,128,128]{2,1,0:T(8,128)S(1)} %get-tuple-element.70), custom_call_target="InvertDiagBlocksLowerTriangular" | custom-call | tf_op jit(solution)/shard_map/jit(_solve_triangular)/triangular_solve | solution.py:110
  (132 shorter events, 53.8 us)
Async XLA Ops:
  7.2 603.3 %all-reduce.3.cloned.1.call-start = ((), (), s32[]{:S(2)}) async-start(), calls=%async_computation | async-start | bytes 131072 | tf_op jit(solution)/shard_map/psum | solution.py:107
  8.5 10.3 %collective-permute-start.3 = (f32[1,16,16,32]{3,2,1,0:T(8,128)S(1)}, f32[1,16,16,32]{3,2,1,0:T(8,128)S(1)}, u32[]{:S(2)}, u32[]{:S(2)}) collective-permute-start(f32[1,16,16,32]{3,2,1,0:T(8,128)S(1)} %get-tuple-element.65), channel_id=1, source_target_pairs={{0,64},{64,128},{128,192},{192,256},{256,320},{320,384},{384,448},... | collective-permute-start | bytes 98312 | tf_op jit(solution)/shard_map/ppermute | solution.py:26
  13.1 6.5 %collective-permute-start.4 = (f32[1,16,16,32]{3,2,1,0:T(8,128)S(1)}, f32[1,16,16,32]{3,2,1,0:T(8,128)S(1)}, u32[]{:S(2)}, u32[]{:S(2)}) collective-permute-start(f32[1,16,16,32]{3,2,1,0:T(8,128)S(1)} %get-tuple-element.66), channel_id=1, source_target_pairs={{64,0},{128,64},{192,128},{256,192},{320,256},{384,320},{448,384},... | collective-permute-start | bytes 98312 | tf_op jit(solution)/shard_map/ppermute | solution.py:29
  18.8 25.6 %copy-start.6 = (f32[1,16,16,32]{3,2,1,0:T(8,128)}, f32[1,16,16,32]{3,2,1,0:T(8,128)S(1)}, u32[]{:S(2)}) copy-start(f32[1,16,16,32]{3,2,1,0:T(8,128)S(1)} %collective-permute-done.3) | copy-start | bytes 98308
  19.6 24.8 %copy-start.7 = (f32[1,16,16,32]{3,2,1,0:T(8,128)}, f32[1,16,16,32]{3,2,1,0:T(8,128)S(1)}, u32[]{:S(2)}) copy-start(f32[1,16,16,32]{3,2,1,0:T(8,128)S(1)} %collective-permute-done.4) | copy-start | bytes 98308
  19.6 7.1 %collective-permute-start.5 = (f32[6,1,16,32]{3,2,1,0:T(8,128)S(1)}, f32[6,1,16,32]{3,2,1,0:T(8,128)S(1)}, u32[]{:S(2)}, u32[]{:S(2)}) collective-permute-start(f32[6,1,16,32]{3,2,1,0:T(8,128)S(1)} %get-tuple-element.59), channel_id=1, source_target_pairs={{0,8},{8,16},{16,24},{24,32},{32,40},{40,48},{48,56},{1,9},{9,17},... | collective-permute-start | bytes 36872 | tf_op jit(solution)/shard_map/ppermute | solution.py:26
  23.4 5.5 collective-permute-start.6
  24.7 17.8 %collective-permute-start = (f32[1,16,16]{2,1,0:T(8,128)S(1)}, f32[1,16,16]{2,1,0:T(8,128)S(1)}, u32[]{:S(2)}, u32[]{:S(2)}) collective-permute-start(f32[1,16,16]{2,1,0:T(8,128)S(1)} %slice_bitcast_fusion.6), channel_id=1, source_target_pairs={{0,64},{64,128},{128,192},{192,256},{256,320},{320,384},{384,448},... | collective-permute-start | bytes 3080 | tf_op jit(solution)/shard_map/ppermute | solution.py:18
  28.9 21.1 %collective-permute-start.7 = (f32[6,18,1,32]{3,2,1,0:T(1,128)S(1)}, f32[6,18,1,32]{3,2,1,0:T(1,128)S(1)}, u32[]{:S(2)}, u32[]{:S(2)}) collective-permute-start(f32[6,18,1,32]{3,2,1,0:T(1,128)S(1)} %get-tuple-element.51), channel_id=1, source_target_pairs={{0,1},{1,2},{2,3},{3,4},{4,5},{5,6},{6,7},{8,9},{9,10},{10,11},{11... | collective-permute-start | bytes 41480 | tf_op jit(solution)/shard_map/ppermute | solution.py:26
  32.2 18.5 %collective-permute-start.8 = (f32[6,18,1,32]{3,2,1,0:T(1,128)S(1)}, f32[6,18,1,32]{3,2,1,0:T(1,128)}, u32[]{:S(2)}, u32[]{:S(2)}) collective-permute-start(f32[6,18,1,32]{3,2,1,0:T(1,128)S(1)} %get-tuple-element.52), channel_id=1, source_target_pairs={{1,0},{2,1},{3,2},{4,3},{5,4},{6,5},{7,6},{9,8},{10,9},{11,10},{12... | collective-permute-start | bytes 41480 | tf_op jit(solution)/shard_map/ppermute | solution.py:29
  33.6 8.8 %collective-permute-start.2 = (f32[4,16,1]{1,0,2:T(4,128)S(1)}, f32[4,16,1]{1,0,2:T(4,128)S(1)}, u32[]{:S(2)}, u32[]{:S(2)}) collective-permute-start(f32[4,16,1]{1,0,2:T(4,128)S(1)} %bitcast.113), channel_id=1, source_target_pairs={{0,1},{1,2},{2,3},{3,4},{4,5},{5,6},{6,7},{8,9},{9,10},{10,11},{11... | collective-permute-start | bytes 776 | tf_op jit(solution)/shard_map/ppermute | solution.py:18
  37.6 5.7 collective-permute-start.1
  52.9 6.3 collective-permute-start.9
  57.3 6.3 collective-permute-start.10
  63.6 6.5 %collective-permute-start.11 = (f32[6,1,16,32]{3,2,1,0:T(8,128)S(1)}, f32[6,1,16,32]{3,2,1,0:T(8,128)S(1)}, u32[]{:S(2)}, u32[]{:S(2)}) collective-permute-start(f32[6,1,16,32]{3,2,1,0:T(8,128)S(1)} %get-tuple-element.57), channel_id=1, source_target_pairs={{0,8},{8,16},{16,24},{24,32},{32,40},{40,48},{48,56},{1,9},{9,17},... | collective-permute-start | bytes 36872 | tf_op jit(solution)/shard_map/ppermute | solution.py:26
  68.8 6.4 %collective-permute-start.12 = (f32[6,1,16,32]{3,2,1,0:T(8,128)S(1)}, f32[6,1,16,32]{3,2,1,0:T(8,128)S(1)}, u32[]{:S(2)}, u32[]{:S(2)}) collective-permute-start(f32[6,1,16,32]{3,2,1,0:T(8,128)S(1)} %get-tuple-element.58), channel_id=1, source_target_pairs={{8,0},{16,8},{24,16},{32,24},{40,32},{48,40},{56,48},{9,1},{17,9},... | collective-permute-start | bytes 36872 | tf_op jit(solution)/shard_map/ppermute | solution.py:29
  75.4 4.5 collective-permute-start.13
  78.6 5.5 collective-permute-start.14
  85.6 6.4 collective-permute-start.15
  90.1 6.3 collective-permute-start.16
  96.4 4.7 collective-permute-start.17
  99.8 5.0 collective-permute-start.18
  104.9 6.2 collective-permute-start.19
  109.8 5.2 collective-permute-start.20
  117.0 27.9 %copy-start.5 = (f32[4,16,1536]{2,1,0:T(8,128)S(1)}, f32[4,16,1536]{2,1,0:T(8,128)}, u32[]{:S(2)}) copy-start(f32[4,16,1536]{2,1,0:T(8,128)} %param.9) | copy-start | bytes 1179652
  117.0 6.8 %collective-permute-start.21 = (f32[1,16,16,32]{3,2,1,0:T(8,128)S(1)}, f32[1,16,16,32]{3,2,1,0:T(8,128)S(1)}, u32[]{:S(2)}, u32[]{:S(2)}) collective-permute-start(f32[1,16,16,32]{3,2,1,0:T(8,128)S(1)} %get-tuple-element.61), channel_id=1, source_target_pairs={{0,64},{64,128},{128,192},{192,256},{256,320},{320,384},{384,448},... | collective-permute-start | bytes 98312 | tf_op jit(solution)/shard_map/ppermute | solution.py:26
  121.8 23.3 %copy-start.4 = (f32[4,16,512]{2,1,0:T(8,128)S(1)}, f32[4,16,512]{2,1,0:T(8,128)}, u32[]{:S(2)}) copy-start(f32[4,16,512]{2,1,0:T(8,128)} %copy-done.3) | copy-start | bytes 393220
  121.8 6.4 collective-permute-start.22
  128.2 6.1 collective-permute-start.23
  133.0 5.4 collective-permute-start.24
  139.2 10.0 %collective-permute-start.25 = (f32[6,18,1,32]{3,2,1,0:T(1,128)}, f32[6,18,1,32]{3,2,1,0:T(1,128)}, u32[]{:S(2)}, u32[]{:S(2)}) collective-permute-start(f32[6,18,1,32]{3,2,1,0:T(1,128)} %get-tuple-element.45), channel_id=1, source_target_pairs={{0,1},{1,2},{2,3},{3,4},{4,5},{5,6},{6,7},{8,9},{9,10},{10,11},{11... | collective-permute-start | bytes 41480 | tf_op jit(solution)/shard_map/ppermute | solution.py:26
  143.4 5.7 collective-permute-start.26
  (12 other events, 85.2 us)
Sparse Core Ops, SparseCore 0:
  355.1 255.3 all-reduce.2
where the time goes:
time: 646 us; the launch traced here: 645 us
  waiting for transfers between devices  292 us (45%)
  blocking collectives  190 us (29%)
  starting transfers between devices  82.5 us (13%)
  other arithmetic  34.8 us (5%)
  local copies, waits for them, and re-layouts  24.4 us (4%)
  between operations  15.5 us (2%)
    psum x1, waiting for transfers between devices, per_device(): lax.psum(jnp.dot(twice.T, twice, precision=PRECISE), ('gx', 'gy', 'gz'))  255 us
    psum x1, blocking collectives, per_device(): lax.psum(jnp.dot(basis_rows.T, krylov, precision=PRECISE), ('gx', 'gy', '...  95.3 us
    psum x1, blocking collectives, per_device(): lax.psum(jnp.dot(basis_rows.T, once, precision=PRECISE), ('gx', 'gy', 'gz'))  94.9 us
    ppermute x12, starting transfers between devices, with_halo(): lax.ppermute(lax.slice_in_dim(block, block.shape[dim] - width, None, axis...  50.5 us
    ppermute x12, waiting for transfers between devices, with_halo(): lax.ppermute(lax.slice_in_dim(block, 0, width, axis=dim), axis, backward)  36.7 us
    ppermute x12, starting transfers between devices, with_halo(): lax.ppermute(lax.slice_in_dim(block, 0, width, axis=dim), axis, backward)  22 us
  transfers between devices with their start and end apart: 28, of which 11 were waited for; matrix products, arithmetic and copies ran while one was open for 2% of the time, Pallas kernels for 0%

commit v1 on v0

v1 whole, which is shorter than its diff:
```python
import functools
import jax
import jax.numpy as jnp
from jax import lax
from jax.experimental import pallas as pl
from jax.experimental.pallas import tpu as pltpu
from jax.sharding import PartitionSpec as P

BLOCK = 32
POWERS = 4
BASIS = 96
LANES = 128
OPERATOR_SCALE = 11.0
CENTRE = 6.0
WIDTH = 2.5
MESH = pl.DeviceIdType.MESH
AXES = ("gx", "gy", "gz")
V_LANE = (64, 32, 0, 96)
V_TILE = (0, 1, 2, 2)


def roll_lanes(values, shift):
    return values if shift % LANES == 0 else pltpu.roll(values, shift % LANES, axis=values.ndim - 1)


def tree_sum(parts):
    while len(parts) > 1:
        parts = [parts[i] + parts[i + 1] for i in range(0, len(parts), 2)]
    return parts[0]


def powers_kernel(
    sizes,
    q_ref,
    w_ref,
    total_ref,
    xa_ref,
    xb_ref,
    field,
    weight,
    coef,
    halo_x,
    halo_y,
    halo_z,
    face_y,
    edge_x,
    edge_y,
    edge_z,
    face_wy,
    local_sum,
    part_x,
    send_z,
    part_z,
    send_y,
    part_y,
    send_x,
    halo_send,
    halo_recv,
    edge_send,
    edge_recv,
    sum_send,
    sum_recv,
):
    nx, ny, nz = sizes
    at = dict(zip(AXES, (lax.axis_index(a) for a in AXES)))
    gx, gy, gz = at["gx"], at["gy"], at["gz"]
    size_of = dict(zip(AXES, sizes))

    def moved(axis, index):
        return tuple(index if a == axis else at[a] for a in AXES)

    def beside(axis, step):
        n = size_of[axis]
        return moved(axis, lax.rem(at[axis] + (n + step), n))

    def partner(axis, d):
        return moved(axis, at[axis] ^ d)

    barrier = pltpu.get_barrier_semaphore()
    peers = 0
    for axis in AXES:
        for d in range(1, size_of[axis]):
            pl.semaphore_signal(barrier, inc=1, device_id=partner(axis, d), device_id_type=MESH)
            peers += 1

    lane = lax.broadcasted_iota(jnp.int32, (16, LANES), 1)
    row = lax.broadcasted_iota(jnp.int32, (16, LANES), 0)
    group = lane // BLOCK

    def by_group(parts):
        out = parts[0]
        for g in range(1, 4):
            out = jnp.where(group == g, parts[g], out)
        return out

    def q_tile(i, n):
        return q_ref[i, :, n * LANES : (n + 1) * LANES]

    def put(level, i, t, value):
        field[level, i, t] = value
        if level < POWERS:
            face_y[level, 0, 4 * i + t : 4 * i + t + 1, :] = value[15:16, :]
            face_y[level, 1, 4 * i + t : 4 * i + t + 1, :] = value[0:1, :]

    for i in range(4):
        for t in range(4):
            put(
                0,
                i,
                t,
                by_group([roll_lanes(q_tile(i, 3 * g + V_TILE[t]), BLOCK * g - V_LANE[t]) for g in range(4)]),
            )

    spread_k = lax.broadcasted_iota(jnp.int32, (16, 4 * LANES), 0)
    spread_lane = lax.broadcasted_iota(jnp.int32, (16, 4 * LANES), 1)
    spread = (spread_k == 4 * ((spread_lane % LANES) // BLOCK) + spread_lane // LANES).astype(jnp.float32)
    wide = jnp.dot(
        w_ref[...].reshape(192, 16), spread, precision=lax.Precision.HIGHEST, preferred_element_type=jnp.float32
    )
    for d in range(3):
        for i in range(4):
            for t in range(4):
                r = 16 * (4 * d + i)
                value = wide[r : r + 16, t * LANES : (t + 1) * LANES] * (1.0 / WIDTH)
                weight[d, i, t] = value
                if d == 1:
                    face_wy[4 * i + t : 4 * i + t + 1, :] = value[15:16, :]

    pl.semaphore_wait(barrier, peers)

    def halo_copies(level):
        def copy(src, dst, n, device):
            return pltpu.make_async_remote_copy(
                src_ref=src,
                dst_ref=dst,
                send_sem=halo_send.at[level, n],
                recv_sem=halo_recv.at[level, n],
                device_id=device,
                device_id_type=MESH,
            )

        return [
            copy(field.at[level, 3], halo_x.at[level, 0], 0, beside("gx", 1)),
            copy(field.at[level, 0], halo_x.at[level, 1], 1, beside("gx", -1)),
            copy(field.at[level, :, 3], halo_z.at[level, 0], 2, beside("gz", 1)),
            copy(field.at[level, :, 0], halo_z.at[level, 1], 3, beside("gz", -1)),
            copy(face_y.at[level, 0], halo_y.at[level, 0], 4, beside("gy", 1)),
            copy(face_y.at[level, 1], halo_y.at[level, 1], 5, beside("gy", -1)),
        ]

    def edge_copy(src, dst, n, axis):
        return pltpu.make_async_remote_copy(
            src_ref=src,
            dst_ref=dst,
            send_sem=edge_send.at[n],
            recv_sem=edge_recv.at[n],
            device_id=beside(axis, 1),
            device_id_type=MESH,
        )

    edges = [
        edge_copy(weight.at[0, 3], edge_x, 0, "gx"),
        edge_copy(weight.at[2, :, 3], edge_z, 1, "gz"),
        edge_copy(face_wy, edge_y, 2, "gy"),
    ]
    rounds = [halo_copies(level) for level in range(POWERS)]
    for copy in edges + rounds[0]:
        copy.start()

    def place_basis():
        for i in range(4):
            for g in range(4):
                a, b, c = (q_tile(i, 3 * g + n) for n in range(3))
                parts = [
                    a,
                    roll_lanes(jnp.where(lane >= 96, a, b), 32),
                    roll_lanes(jnp.where(lane >= 64, b, c), 64),
                    roll_lanes(c, 96),
                ]
                for t in range(4):
                    xa_ref[4 * g + t, 16 * i : 16 * i + 16, :] = parts[t]

    place_basis()

    for copy in edges:
        copy.wait_recv()
    low_x, high_x = gx > 0, gx < nx - 1
    low_y, high_y = gy > 0, gy < ny - 1
    low_z, high_z = gz > 0, gz < nz - 1

    def kept(flag):
        return jnp.where(flag, 1.0, 0.0).astype(jnp.float32)

    for i in range(4):
        for t in range(4):
            xp, yp, zp = weight[0, i, t], weight[1, i, t], weight[2, i, t]
            xm = weight[0, i - 1, t] if i > 0 else edge_x[t] * kept(low_x)
            ym = jnp.where(
                row == 0, edge_y[4 * i + t : 4 * i + t + 1, :] * kept(low_y), pltpu.roll(yp, 1, axis=0)
            )
            if t > 0:
                zm = weight[2, i, t - 1]
            else:
                zm = jnp.where(
                    group == 0, roll_lanes(edge_z[i], 32) * kept(low_z), roll_lanes(weight[2, i, 3], 32)
                )
            coef[0, i, t] = ((xp + xm) + (yp + ym)) + (zp + zm) - CENTRE / WIDTH
            coef[1, i, t] = xp * kept(high_x) if i == 3 else xp
            coef[2, i, t] = xm
            coef[3, i, t] = jnp.where(row == 15, yp * kept(high_y), yp)
            coef[4, i, t] = ym
            coef[5, i, t] = jnp.where(group == 3, zp * kept(high_z), zp) if t == 3 else zp
            coef[6, i, t] = zm

    for level in range(POWERS):
        for copy in rounds[level]:
            copy.wait_recv()
        for i in range(4):
            for t in range(4):
                centre = field[level, i, t]
                xp = field[level, i + 1, t] if i < 3 else halo_x[level, 1, t]
                xm = field[level, i - 1, t] if i > 0 else halo_x[level, 0, t]
                r = 4 * i + t
                yp = jnp.where(row == 15, halo_y[level, 1, r : r + 1, :], pltpu.roll(centre, 15, axis=0))
                ym = jnp.where(row == 0, halo_y[level, 0, r : r + 1, :], pltpu.roll(centre, 1, axis=0))
                if t < 3:
                    zp = field[level, i, t + 1]
                else:
                    zp = roll_lanes(jnp.where(group == 0, halo_z[level, 1, i], field[level, i, 0]), 96)
                if t > 0:
                    zm = field[level, i, t - 1]
                else:
                    zm = roll_lanes(jnp.where(group == 3, halo_z[level, 0, i], field[level, i, 3]), 32)
                value = coef[0, i, t] * centre
                value = value - (coef[1, i, t] * xp + coef[2, i, t] * xm)
                value = value - (coef[3, i, t] * yp + coef[4, i, t] * ym)
                value = value - (coef[5, i, t] * zp + coef[6, i, t] * zm)
                if level > 0:
                    value = value - field[level - 1, i, t]
                put(level + 1, i, t, value)
        if level + 1 < POWERS:
            for copy in rounds[level + 1]:
                copy.start()

    zero = jnp.zeros((16, LANES), jnp.float32)
    for i in range(4):
        for g in range(4):
            for t in range(4):
                k = 4 * g + t
                rows = slice(16 * i, 16 * i + 16)
                pieces = [roll_lanes(field[m + 1, i, t], BLOCK * (m - g)) for m in range(4)]
                xa_ref[k, rows, :] = jnp.where(group == 3, pieces[3], xa_ref[k, rows, :])
                xb_ref[k, rows, :] = by_group(pieces[:3] + [zero])

    xa = xa_ref[...].reshape(1024, LANES)
    xb = xb_ref[...].reshape(1024, LANES)
    both = jnp.concatenate([xa, xb], axis=1)
    gram = lax.dot_general(
        xa,
        both,
        (((0,), (0,)), ((), ())),
        precision=lax.Precision.HIGH,
        preferred_element_type=jnp.float32,
    )
    chunk = LANES // nx
    for c in range(nx):
        local_sum[c] = gram[c * chunk : (c + 1) * chunk, :]

    def sum_copy(src, dst, n, device):
        return pltpu.make_async_remote_copy(
            src_ref=src,
            dst_ref=dst,
            send_sem=sum_send.at[n],
            recv_sem=sum_recv.at[n],
            device_id=device,
            device_id_type=MESH,
        )

    for d in range(1, nx):
        sum_copy(local_sum.at[gx ^ d], part_x.at[d], 0, partner("gx", d)).start()
    part_x[0] = local_sum[gx]
    all_x = sum_copy(part_x.at[pl.ds(1, nx - 1)], part_x.at[pl.ds(1, nx - 1)], 0, partner("gx", 1))
    all_x.wait_recv()
    send_z[...] = tree_sum([part_x[d] for d in range(nx)])
    for d in range(1, nz):
        sum_copy(send_z, part_z.at[d], 1, partner("gz", d)).start()
    all_z = sum_copy(part_z.at[pl.ds(1, nz - 1)], part_z.at[pl.ds(1, nz - 1)], 1, partner("gz", 1))
    all_z.wait_recv()
    send_y[...] = tree_sum([send_z[...]] + [part_z[d] for d in range(1, nz)])
    for d in range(1, ny):
        sum_copy(send_y, part_y.at[d], 2, partner("gy", d)).start()
    all_y = sum_copy(part_y.at[pl.ds(1, ny - 1)], part_y.at[pl.ds(1, ny - 1)], 2, partner("gy", 1))
    all_y.wait_recv()
    whole = tree_sum([send_y[...]] + [part_y[d] for d in range(1, ny)])
    send_x[...] = whole
    for d in range(1, nx):
        sum_copy(send_x, total_ref.at[gx], 3, partner("gx", d)).start()
    total_ref[gx] = whole
    last = sum_copy(total_ref.at[pl.ds(0, nx - 1)], total_ref.at[pl.ds(0, nx - 1)], 3, partner("gx", 1))
    last.wait_recv()

    for copy in edges + [c for r in rounds for c in r]:
        copy.wait_send()
    for copy in (all_x, all_z, all_y, last):
        copy.wait_send()


def basis_kernel(cells, total_ref, xa_ref, xb_ref, shift_ref, new_ref, projection_ref, triangle_ref, factor, inverse):
    exact = functools.partial(
        lax.dot_general, precision=lax.Precision.HIGHEST, preferred_element_type=jnp.float32
    )

    def mm(a, b):
        return exact(a, b, (((1,), (0,)), ((), ())))

    alpha = WIDTH / OPERATOR_SCALE
    beta = (shift_ref[0] + CENTRE) / OPERATOR_SCALE - 1.0
    t = [[1.0, 0.0, 0.0, 0.0, 0.0], [beta, alpha, 0.0, 0.0, 0.0]]
    for k in range(1, POWERS):
        p, before = t[k], t[k - 1]
        nxt = []
        for j in range(5):
            if j > k + 1:
                nxt.append(0.0)
                continue
            shifted = (p[j - 1] if j > 0 else 0.0) + (p[j + 1] if j < 4 else 0.0)
            nxt.append(2.0 * (alpha * shifted + beta * p[j]) - before[j])
        t.append(nxt)
    tau = []
    for k in range(1, POWERS + 1):
        rest = t[k][0]
        for j in range(1, k):
            rest = rest - t[k][j] * tau[j - 1]
        tau.append(rest * (1.0 / (alpha * (2.0 * alpha) ** (k - 1))))

    def lanes_of(shape):
        return lax.broadcasted_iota(jnp.int32, shape, 1)

    def by_group(shape, values, dim=1):
        which = lax.broadcasted_iota(jnp.int32, shape, dim) // BLOCK
        out = jnp.full(shape, values[0], jnp.float32)
        for n in range(1, 4):
            out = jnp.where(which == n, values[n], out)
        return out

    scale = 1.0 / cells
    left = total_ref[...].reshape(LANES, 2 * LANES)[:, :LANES] * scale
    right = total_ref[...].reshape(LANES, 2 * LANES)[:, LANES:] * scale
    merged = jnp.where(lanes_of((LANES, LANES)) < BASIS, right, left)
    gram_q = left[:BASIS, :]
    coef = merged[:BASIS, :]
    last = merged[BASIS:, :]

    strip = lanes_of((BLOCK, LANES))
    rows = [coef[64:96, :]]
    moment = [roll_lanes(gram_q[64:96, :], 64)] + [roll_lanes(rows[0], -BLOCK * m) for m in range(3)]
    for j in range(POWERS - 1):
        up = roll_lanes(rows[j], -BLOCK)
        down = jnp.where(strip < BLOCK, moment[j], roll_lanes(rows[j], BLOCK))
        nxt = up + down
        if j > 0:
            nxt = nxt - rows[j - 1]
        rows.append(jnp.where(strip < BASIS, nxt, roll_lanes(last, BASIS - BLOCK * j)))
    gram_b = jnp.concatenate(rows[1:] + [last], axis=0)

    wide = lanes_of((BASIS, LANES))
    tall = lax.broadcasted_iota(jnp.int32, (BASIS, LANES), 0)
    off = jnp.where(wide < BASIS, jnp.where(wide == tall, 1.0, 0.0) - gram_q, 0.0)
    e1 = off[:, :BASIS]
    first = mm(e1, jnp.concatenate([off, coef], axis=1))
    square, c2 = first[:, :LANES], first[:, LANES:]
    e2 = square[:, :BASIS]
    second = mm(e2, jnp.concatenate([coef, c2, square], axis=1))
    c3, c4, fourth = second[:, :LANES], second[:, LANES : 2 * LANES], second[:, 2 * LANES :]
    left_over = mm(fourth[64:96, :BASIS], jnp.concatenate([coef, gram_q], axis=1))
    over_b, over_v = left_over[:, :LANES], left_over[:, LANES:]
    gram = gram_b - exact(coef, (coef + c2) + (c3 + c4), (((0,), (0,)), ((), ())))
    over_v = roll_lanes(over_v, -64)
    over_v = jnp.where(strip < BLOCK, over_v, 0.0)
    over_v = (over_v + roll_lanes(over_v, 32)) + (roll_lanes(over_v, 64) + roll_lanes(over_v, 96))
    half = over_b + (0.5 * by_group((BLOCK, LANES), tau)) * over_v
    half = jnp.concatenate([tau[n] * half for n in range(4)], axis=0)
    gram = gram + (half + half.T)

    sub = lax.broadcasted_iota(jnp.int32, (8, LANES), 0)
    lane8 = lanes_of((8, LANES))
    a = [gram[8 * b : 8 * b + 8, :] for b in range(16)]
    z = [jnp.where(lane8 == sub + 8 * b, 1.0, 0.0) for b in range(16)]
    for j in range(LANES):
        b0, s = divmod(j, 8)
        row_a, row_z = a[b0][s : s + 1, :], z[b0][s : s + 1, :]
        pivot = row_a[:, j : j + 1]
        root = lax.rsqrt(pivot)
        row_a, row_z = row_a * root, row_z * root
        factor[j : j + 1, :] = row_a
        inverse[j : j + 1, :] = row_z
        for b in range(b0, 16):
            if b == b0 and s == 7:
                continue
            column = a[b][:, j : j + 1] * root
            if b == b0:
                column = jnp.where(sub > s, column, 0.0)
            a[b] = a[b] - column * row_a
            z[b] = z[b] - column * row_z

    square_lane = lanes_of((LANES, LANES))
    square_row = lax.broadcasted_iota(jnp.int32, (LANES, LANES), 0)
    upper = jnp.where(square_lane >= square_row, factor[...], 0.0)
    lower_inverse = jnp.where(square_lane <= square_row, inverse[...], 0.0)

    t_rows = [by_group((LANES, LANES), [t[k][j] for k in range(1, 5)]) for j in range(1, 5)]
    which = square_row // BLOCK
    mixing = t_rows[0]
    for n in range(1, 4):
        mixing = jnp.where(which == n, t_rows[n], mixing)
    mixing = jnp.where(square_row % BLOCK == square_lane % BLOCK, mixing, 0.0)
    triangle_ref[...] = jnp.where(square_lane >= square_row, mm(upper, mixing), 0.0)

    twice = coef + c2
    leak = jnp.where(wide < BLOCK, roll_lanes(square, -64), 0.0)
    leak = (leak + roll_lanes(leak, 32)) + (roll_lanes(leak, 64) + roll_lanes(leak, 96))
    unit = jnp.where(tall - 64 == wide % BLOCK, 1.0, 0.0)
    projection_ref[...] = mm(twice, mixing) + by_group((BASIS, LANES), [t[k][0] for k in range(1, 5)]) * (unit - leak)

    back = leak * by_group((BASIS, LANES), tau) - twice
    back = exact(back, lower_inverse, (((1,), (1,)), ((), ())))
    upper_inverse = lower_inverse.T
    maps = jnp.concatenate([back, upper_inverse[BASIS:, :], upper_inverse], axis=0)
    for k in range(16):
        both = jnp.concatenate([xa_ref[k], xb_ref[k]], axis=1)
        out = lax.dot_general(
            both,
            maps,
            (((1,), (0,)), ((), ())),
            precision=lax.Precision.HIGH,
            preferred_element_type=jnp.float32,
        )
        for i in range(4):
            new_ref[i, :, k * LANES : (k + 1) * LANES] = out[16 * i : 16 * i + 16, :]


def per_device(sizes, prior_basis, edge_weights, spectral_shift):
    nx, ny, nz = sizes
    f32 = jnp.float32
    chunk = LANES // nx
    piece = (chunk, 2 * LANES)
    vmem = pl.BlockSpec(memory_space=pltpu.VMEM)
    total, xa, xb = pl.pallas_call(
        functools.partial(powers_kernel, sizes),
        out_shape=(
            jax.ShapeDtypeStruct((nx, *piece), f32),
            jax.ShapeDtypeStruct((16, 64, LANES), f32),
            jax.ShapeDtypeStruct((16, 64, LANES), f32),
        ),
        in_specs=[vmem, vmem],
        out_specs=(vmem, vmem, vmem),
        scratch_shapes=[
            pltpu.VMEM((POWERS + 1, 4, 4, 16, LANES), f32),
            pltpu.VMEM((3, 4, 4, 16, LANES), f32),
            pltpu.VMEM((7, 4, 4, 16, LANES), f32),
            pltpu.VMEM((POWERS, 2, 4, 16, LANES), f32),
            pltpu.VMEM((POWERS, 2, 16, LANES), f32),
            pltpu.VMEM((POWERS, 2, 4, 16, LANES), f32),
            pltpu.VMEM((POWERS, 2, 16, LANES), f32),
            pltpu.VMEM((4, 16, LANES), f32),
            pltpu.VMEM((16, LANES), f32),
            pltpu.VMEM((4, 16, LANES), f32),
            pltpu.VMEM((16, LANES), f32),
            pltpu.VMEM((nx, *piece), f32),
            pltpu.VMEM((nx, *piece), f32),
            pltpu.VMEM(piece, f32),
            pltpu.VMEM((nz, *piece), f32),
            pltpu.VMEM(piece, f32),
            pltpu.VMEM((ny, *piece), f32),
            pltpu.VMEM(piece, f32),
            pltpu.SemaphoreType.DMA((POWERS, 6)),
            pltpu.SemaphoreType.DMA((POWERS, 6)),
            pltpu.SemaphoreType.DMA((3,)),
            pltpu.SemaphoreType.DMA((3,)),
            pltpu.SemaphoreType.DMA((4,)),
            pltpu.SemaphoreType.DMA((4,)),
        ],
        name="powers",
        compiler_params=pltpu.CompilerParams(
            collective_id=0, has_side_effects=True, vmem_limit_bytes=32 * 2**20
        ),
    )(prior_basis, edge_weights)
    cells = 1024 * nx * ny * nz
    return pl.pallas_call(
        functools.partial(basis_kernel, cells),
        out_shape=(
            jax.ShapeDtypeStruct((4, 16, 16 * LANES), f32),
            jax.ShapeDtypeStruct((BASIS, LANES), f32),
            jax.ShapeDtypeStruct((LANES, LANES), f32),
        ),
        in_specs=[vmem, vmem, vmem, pl.BlockSpec(memory_space=pltpu.SMEM)],
        out_specs=(vmem, vmem, vmem),
        scratch_shapes=[pltpu.VMEM((LANES, LANES), f32), pltpu.VMEM((LANES, LANES), f32)],
        name="basis",
        compiler_params=pltpu.CompilerParams(vmem_limit_bytes=32 * 2**20),
    )(total, xa, xb, spectral_shift)


def solution(mesh):
    sizes = tuple(mesh.shape[a] for a in AXES)
    return jax.shard_map(
        functools.partial(per_device, sizes),
        mesh=mesh,
        in_specs=(P("gx", "gy", "gz"), P(None, "gx", "gy", "gz"), P()),
        out_specs=(P("gx", "gy", "gz"), P(), P()),
        check_vma=False,
    )
```

time: 646 us -> 67.2 us (0.10)
  waiting for transfers between devices: 292 us -> 0 us
  blocking collectives: 190 us -> 0 us
  starting transfers between devices: 82.5 us -> 0 us
  Pallas kernels: 0 us -> 63.8 us
  other arithmetic: 34.8 us -> 0 us
  local copies, waits for them, and re-layouts: 24.4 us -> 1.88 us
  between operations: 15.5 us -> 1.29 us
    psum x1 -> x0, waiting for transfers between devices: 255 us -> none  [per_device(): lax.psum(jnp.dot(twice.T, twice, precision=PRECISE), ('gx', 'gy', 'gz'))]
    psum x2 -> x0, blocking collectives: 190 us -> none  [the longest x1 95.3 us: per_device(): lax.psum(jnp.dot(basis_rows.T, krylov, precision=PRECISE), ('gx', 'gy', '...]
    ppermute x27 -> x0, starting transfers between devices: 82.5 us -> none  [the longest x12 50.5 us: with_halo(): lax.ppermute(lax.slice_in_dim(block, block.shape[dim] - width, None, axis...]
    pallas_call x0 -> x2, Pallas kernels: none -> 63.8 us  [the longest x1 50.3 us: per_device(): pl.pallas_call(functools.partial(powers_kernel, sizes), out_shape=(jax.Sh...]
    ppermute x27 -> x0, waiting for transfers between devices: 36.8 us -> none  [the longest x12 36.7 us: with_halo(): lax.ppermute(lax.slice_in_dim(block, 0, width, axis=dim), axis, backward)]
    another operation x6 -> x0, other arithmetic: 22.5 us -> none  [the longest x3 12.4 us: per_device(): lower_factor = jnp.linalg.cholesky(gram_matrix)]
    reshape x11 -> x0, local copies, waits for them, and re-layouts: 10.8 us -> none  [the longest x1 3.12 us: per_device(): weight_pad = jnp.repeat(weight_pad, BLOCK, axis=3)]
  transfers between devices with their start and end apart: 28 -> 0, of which waited for: 11 -> 0; matrix products, arithmetic and copies ran while one was open for 2% -> 0% of each run, Pallas kernels for 0% -> 0%
where the time goes in v1:
time: 67.2 us; the launch traced here: 67 us
  Pallas kernels  63.8 us (95%)
  local copies, waits for them, and re-layouts  1.88 us (3%)
  between operations  1.29 us (2%)
    pallas_call x1, Pallas kernels, per_device(): pl.pallas_call(functools.partial(powers_kernel, sizes), out_shape=(jax.Sh...  50.3 us
    pallas_call x1, Pallas kernels, per_device(): pl.pallas_call(functools.partial(basis_kernel, cells), out_shape=(jax.Sha...  13.5 us
    unnamed x4, local copies, waits for them, and re-layouts  1.88 us

profile of v1, /device:TPU:1, one launch (start us, length us, event | category | flops | bytes accessed | tf_op | source)
XLA Modules:
  0.0 67.0 jit_solution(5052683144204737935)
XLA Ops:
  1.3 0.0 copy-start
  1.3 1.0 %copy-done = f32[4,16,1536]{2,1,0:T(8,128)S(1)} copy-done((f32[4,16,1536]{2,1,0:T(8,128)S(1)}, f32[4,16,1536]{2,1,0:T(8,128)}, u32[]{:S(2)}) %copy-start) | copy-done | bytes 393240
  2.3 0.0 copy-start.1
  2.3 0.9 %copy-done.1 = f32[3,4,16,16]{3,2,1,0:T(8,128)S(1)} copy-done((f32[3,4,16,16]{3,2,1,0:T(8,128)S(1)}, f32[3,4,16,16]{3,2,1,0:T(8,128)}, u32[]{:S(2)}) %copy-start.1) | copy-done | bytes 12312
  3.2 50.3 %powers.1 = (f32[8,16,256]{2,1,0:T(8,128)S(1)}, f32[16,64,128]{2,1,0:T(8,128)S(1)}, f32[16,64,128]{2,1,0:T(8,128)S(1)}) custom-call(f32[4,16,1536]{2,1,0:T(8,128)S(1)} %copy-done, f32[3,4,16,16]{3,2,1,0:T(8,128)S(1)} %copy-done.1), custom_call_target="tpu_custom_call" | custom-call | tf_op jit(solution)/shard_map/powers/pallas_call | solution.py:448
  53.5 13.5 %basis.1 = (f32[4,16,2048]{2,1,0:T(8,128)}, f32[96,128]{1,0:T(8,128)}, f32[128,128]{1,0:T(8,128)}) custom-call(f32[8,16,256]{2,1,0:T(8,128)S(1)} %get-tuple-element.6.total_ref, f32[16,64,128]{2,1,0:T(8,128)S(1)} %get-tuple-element.7.xa_ref, f32[16,64,128]{2,1,0:T(8,128)S(1)} %get-tuple-element.8.xb_ref, f32[1]{0:T(128)S(6)} %copy.6.shift_ref), custom_call_target="tpu_custom_call" | custom-call | tf_op jit(solution)/shard_map/basis/pallas_call | solution.py:489
Async XLA Ops:
  1.3 1.0 %copy-start = (f32[4,16,1536]{2,1,0:T(8,128)S(1)}, f32[4,16,1536]{2,1,0:T(8,128)}, u32[]{:S(2)}) copy-start(f32[4,16,1536]{2,1,0:T(8,128)} %q_ref.1) | copy-start | bytes 1179652
  2.3 0.9 %copy-start.1 = (f32[3,4,16,16]{3,2,1,0:T(8,128)S(1)}, f32[3,4,16,16]{3,2,1,0:T(8,128)}, u32[]{:S(2)}) copy-start(f32[3,4,16,16]{3,2,1,0:T(8,128)} %w_ref.1) | copy-start | bytes 36868

commit v2 on v1

v2 whole, which is shorter than its diff:
```python
import functools
import jax
import jax.numpy as jnp
from jax import lax
from jax.experimental import pallas as pl
from jax.experimental.pallas import tpu as pltpu
from jax.sharding import PartitionSpec as P

BLOCK = 32
POWERS = 4
BASIS = 96
LANES = 128
OPERATOR_SCALE = 11.0
CENTRE = 6.0
WIDTH = 2.5
MESH = pl.DeviceIdType.MESH
AXES = ("gx", "gy", "gz")
V_LANE = (64, 32, 0, 96)
V_TILE = (0, 1, 2, 2)


def roll_lanes(values, shift):
    return values if shift % LANES == 0 else pltpu.roll(values, shift % LANES, axis=values.ndim - 1)


def tree_sum(parts):
    while len(parts) > 1:
        parts = [parts[i] + parts[i + 1] for i in range(0, len(parts), 2)]
    return parts[0]


def exact(a, b, dims):
    return lax.dot_general(
        a, b, (dims, ((), ())), precision=lax.Precision.HIGHEST, preferred_element_type=jnp.float32
    )


def mm(a, b):
    return exact(a, b, ((1,), (0,)))


def mm_t(a, b):
    return exact(a, b, ((1,), (1,)))


def lanes_of(shape):
    return lax.broadcasted_iota(jnp.int32, shape, 1)


def rows_of(shape):
    return lax.broadcasted_iota(jnp.int32, shape, 0)


def by_block(shape, values, dim=1):
    which = lax.broadcasted_iota(jnp.int32, shape, dim) // BLOCK
    out = jnp.full(shape, values[0], jnp.float32)
    for n in range(1, 4):
        out = jnp.where(which == n, values[n], out)
    return out


def pick(parts):
    shape = next(p.shape for p in parts if p is not None)
    which = lanes_of(shape) // BLOCK
    out = jnp.zeros(shape, jnp.float32)
    for n, p in enumerate(parts):
        if p is not None:
            out = jnp.where(which == n, p, out)
    return out


def spread_block(values, block):
    own = jnp.where(lanes_of(values.shape) // BLOCK == block, values, 0.0)
    own = own + roll_lanes(own, 32)
    return own + roll_lanes(own, 64)


def scalars(shift):
    alpha = WIDTH / OPERATOR_SCALE
    beta = (shift + CENTRE) / OPERATOR_SCALE - 1.0
    t = [[1.0, 0.0, 0.0, 0.0, 0.0], [beta, alpha, 0.0, 0.0, 0.0]]
    for k in range(1, POWERS):
        p, before = t[k], t[k - 1]
        row = []
        for j in range(5):
            if j > k + 1:
                row.append(0.0)
                continue
            shifted = (p[j - 1] if j > 0 else 0.0) + (p[j + 1] if j < 4 else 0.0)
            row.append(2.0 * (alpha * shifted + beta * p[j]) - before[j])
        t.append(row)
    tau = []
    for k in range(1, POWERS + 1):
        rest = t[k][0]
        for j in range(1, k):
            rest = rest - t[k][j] * tau[j - 1]
        tau.append(rest * (1.0 / (alpha * (2.0 * alpha) ** (k - 1))))
    return t, tau


def prior_algebra(gram, tau):
    shape = (LANES, LANES)
    lane, row = lanes_of(shape), rows_of(shape)
    inside = (lane >= BLOCK) & (row >= BLOCK)
    prior = jnp.where(inside, gram, 0.0)
    unit = jnp.where(inside & (lane == row), 1.0, 0.0)
    off = unit - prior
    off2 = mm(off, off)
    high = mm(off2, jnp.concatenate([off, off2], axis=1))
    off3, off4 = high[:, :LANES], high[:, LANES:]
    series = (unit + off) + (off2 + off3)
    tau_row = by_block((1, LANES), tau)
    right = jnp.concatenate([series, spread_block(off4, 1) * tau_row, unit + off], axis=1)
    over = off4[32:64, :]
    over_v = mm(over, spread_block(prior, 1) * tau_row)
    return dict(right=right, over=over, over_v=over_v, off2=off2)


def level_algebra(m, products, p, done, prior, tau, eliminate):
    strip = (BLOCK, LANES)
    lane, row = lanes_of(strip), rows_of(strip)
    p[2 * m] = (products, 0)
    p[2 * m - 1] = (products, 1)

    def at(n, block):
        values, own = p[n]
        return roll_lanes(values, BLOCK * (block - own))

    moment = at(m, 1) - at(m - 2, 1) if m > 1 else at(1, 1)
    coef = pick([None, moment, products, products])
    mixed = mm(coef, prior["right"])
    series, over, twice = mixed[:, :LANES], mixed[:, LANES : 2 * LANES], mixed[:, 2 * LANES :]
    blocks = [None] * 4
    for k in range(1, m + 1):
        value = at(m + k, k - 1)
        if m - k >= 2:
            value = value - at(m - k - 2, k - 1)
        blocks[k - 1] = value
    nothing = jnp.zeros(strip, jnp.float32)

    def column(name, own):
        parts = done[name] + [own]
        return jnp.concatenate(parts + [nothing] * (4 - len(parts)), axis=0)

    coefs = column("coef", coef)
    inverse = column("inverse", nothing)
    gram = pick(blocks) + over + tau[m - 1] * prior["over_v"]
    gram = gram + mm_t(tau[m - 1] * prior["over"] - series, coefs)
    below = roll_lanes(gram, -BLOCK * (m - 1))
    if m > 1:
        factor = mm_t(gram, inverse)
        pad = jnp.concatenate([factor] + [nothing] * 3, axis=0)
        below = below - mm_t(factor, pad)
        product = mm(factor, inverse)
    work = jnp.where(lane < BLOCK, below, jnp.where(lane == row + BLOCK, 1.0, 0.0))
    work = eliminate(work)
    upper = jnp.where((lane < BLOCK) & (lane >= row), work, 0.0)
    lower = jnp.where((lane >= BLOCK) & (lane <= row + BLOCK), work, 0.0)
    inverse_row = roll_lanes(lower, BLOCK * (m - 2))
    if m > 1:
        pad = jnp.concatenate([product] + [nothing] * 3, axis=0)
        inverse_row = inverse_row - mm(roll_lanes(lower, -BLOCK), pad)
    else:
        factor = nothing
    back = tau[m - 1] * prior["off2"][32:64, :] - twice
    back_row = mm(inverse_row, column("back", back))
    left = pick([roll_lanes(inverse_row, -32), roll_lanes(inverse_row, 32), back_row, back_row])
    right = pick([roll_lanes(inverse_row, 32), roll_lanes(inverse_row, -32), roll_lanes(back_row, 32), None])
    done["coef"].append(coef)
    done["inverse"].append(inverse_row)
    done["back"].append(back)
    return dict(
        maps=jnp.concatenate([left, right], axis=1),
        factor=factor,
        upper=roll_lanes(upper, BLOCK * (m - 1)),
        twice=twice,
    )


def mixing_of(t):
    shape = (LANES, LANES)
    lane, row = lanes_of(shape), rows_of(shape)
    out = jnp.zeros(shape, jnp.float32)
    for j in range(1, 5):
        out = jnp.where(row // BLOCK == j - 1, by_block(shape, [t[k][j] for k in range(1, 5)]), out)
    return jnp.where(row % BLOCK == lane % BLOCK, out, 0.0)


def small_outputs(factor, upper, twice, off2, t):
    shape = (LANES, LANES)
    lane, row = lanes_of(shape), rows_of(shape)
    mixing = mixing_of(t)
    triangle = jnp.where(lane >= row, mm(upper + factor.T, mixing), 0.0)
    unit = jnp.where((row // BLOCK == 1) & (row % BLOCK == lane % BLOCK), 1.0, 0.0)
    start = by_block(shape, [t[k][0] for k in range(1, 5)]) * (unit - spread_block(off2, 1))
    projection = exact(twice, mixing, ((0,), (0,))) + start
    return projection, triangle


def eliminate_in(rows_ref):
    def run(work):
        sub = rows_of((8, LANES))
        a = [work[8 * b : 8 * b + 8, :] for b in range(4)]
        for j in range(BLOCK):
            b0, s = divmod(j, 8)
            row = a[b0][s : s + 1, :]
            root = lax.rsqrt(row[:, j : j + 1])
            row = row * root
            rows_ref[j : j + 1, :] = row
            for b in range(b0, 4):
                if b == b0 and s == 7:
                    continue
                column = a[b][:, j : j + 1] * root
                if b == b0:
                    column = jnp.where(sub > s, column, 0.0)
                a[b] = a[b] - column * row
        return rows_ref[...]

    return run


def powers_kernel(
    sizes,
    q_hbm,
    w_hbm,
    shift_ref,
    xa_ref,
    xb_ref,
    maps_ref,
    small_ref,
    q_ref,
    w_ref,
    y_ref,
    field,
    weight,
    coef,
    halo_x,
    halo_y,
    halo_z,
    face_y,
    edge_x,
    edge_y,
    edge_z,
    face_wy,
    rows_ref,
    gathered,
    stream_a,
    stream_2,
    stream_3,
    stream_4,
    load_sem,
    halo_send,
    halo_recv,
    edge_send,
    edge_recv,
    sum_send,
    sum_recv,
):
    nx, ny, nz = sizes
    at = dict(zip(AXES, (lax.axis_index(a) for a in AXES)))
    gx, gy, gz = at["gx"], at["gy"], at["gz"]
    size_of = dict(zip(AXES, sizes))

    def moved(axis, index):
        return tuple(index if a == axis else at[a] for a in AXES)

    def beside(axis, step):
        n = size_of[axis]
        return moved(axis, lax.rem(at[axis] + (n + step), n))

    def partner(axis, d):
        return moved(axis, at[axis] ^ d)

    loads = [
        pltpu.make_async_copy(q_hbm, q_ref, load_sem.at[0]),
        pltpu.make_async_copy(w_hbm, w_ref, load_sem.at[1]),
    ]
    for copy in loads:
        copy.start()

    barrier = pltpu.get_barrier_semaphore()
    peers = 0
    for axis in AXES:
        for d in range(1, size_of[axis]):
            pl.semaphore_signal(barrier, inc=1, device_id=partner(axis, d), device_id_type=MESH)
            peers += 1

    lane = lax.broadcasted_iota(jnp.int32, (16, LANES), 1)
    row = lax.broadcasted_iota(jnp.int32, (16, LANES), 0)
    group = lane // BLOCK

    def q_tile(i, n):
        return q_ref[i, :, n * LANES : (n + 1) * LANES]

    def put(level, i, t, value):
        field[level, i, t] = value
        if level < POWERS:
            face_y[level, 0, 4 * i + t : 4 * i + t + 1, :] = value[15:16, :]
            face_y[level, 1, 4 * i + t : 4 * i + t + 1, :] = value[0:1, :]

    for copy in loads:
        copy.wait()
    for i in range(4):
        for t in range(4):
            put(
                0,
                i,
                t,
                pick([roll_lanes(q_tile(i, 3 * g + V_TILE[t]), BLOCK * g - V_LANE[t]) for g in range(4)]),
            )

    spread_k = lax.broadcasted_iota(jnp.int32, (16, 4 * LANES), 0)
    spread_lane = lax.broadcasted_iota(jnp.int32, (16, 4 * LANES), 1)
    spread = (spread_k == 4 * ((spread_lane % LANES) // BLOCK) + spread_lane // LANES).astype(jnp.float32)
    wide = jnp.dot(
        w_ref[...].reshape(192, 16), spread, precision=lax.Precision.HIGHEST, preferred_element_type=jnp.float32
    )
    for d in range(3):
        for i in range(4):
            for t in range(4):
                r = 16 * (4 * d + i)
                value = wide[r : r + 16, t * LANES : (t + 1) * LANES] * (1.0 / WIDTH)
                weight[d, i, t] = value
                if d == 1:
                    face_wy[4 * i + t : 4 * i + t + 1, :] = value[15:16, :]

    pl.semaphore_wait(barrier, peers)

    def halo_copies(level):
        def copy(src, dst, n, device):
            return pltpu.make_async_remote_copy(
                src_ref=src,
                dst_ref=dst,
                send_sem=halo_send.at[level, n],
                recv_sem=halo_recv.at[level, n],
                device_id=device,
                device_id_type=MESH,
            )

        return [
            copy(field.at[level, 3], halo_x.at[level, 0], 0, beside("gx", 1)),
            copy(field.at[level, 0], halo_x.at[level, 1], 1, beside("gx", -1)),
            copy(field.at[level, :, 3], halo_z.at[level, 0], 2, beside("gz", 1)),
            copy(field.at[level, :, 0], halo_z.at[level, 1], 3, beside("gz", -1)),
            copy(face_y.at[level, 0], halo_y.at[level, 0], 4, beside("gy", 1)),
            copy(face_y.at[level, 1], halo_y.at[level, 1], 5, beside("gy", -1)),
        ]

    def edge_copy(src, dst, n, axis):
        return pltpu.make_async_remote_copy(
            src_ref=src,
            dst_ref=dst,
            send_sem=edge_send.at[n],
            recv_sem=edge_recv.at[n],
            device_id=beside(axis, 1),
            device_id_type=MESH,
        )

    edges = [
        edge_copy(weight.at[0, 3], edge_x, 0, "gx"),
        edge_copy(weight.at[2, :, 3], edge_z, 1, "gz"),
        edge_copy(face_wy, edge_y, 2, "gy"),
    ]
    rounds = [halo_copies(level) for level in range(POWERS)]
    for copy in edges + rounds[0]:
        copy.start()

    for i in range(4):
        rows = slice(16 * i, 16 * i + 16)
        for g in range(4):
            a, b, c = (q_tile(i, 3 * g + n) for n in range(3))
            pairs = [
                roll_lanes(a, 64),
                roll_lanes(jnp.where(lane >= 96, a, b), 96),
                b,
                roll_lanes(c, 32),
            ]
            for t in range(4):
                y_ref[4 * g + t, rows, :] = pairs[t]
                xb_ref[4 * g + t, rows, :] = roll_lanes(field[0, i, t], BLOCK * (2 - g))

    for copy in edges:
        copy.wait_recv()
    low_x, high_x = gx > 0, gx < nx - 1
    low_y, high_y = gy > 0, gy < ny - 1
    low_z, high_z = gz > 0, gz < nz - 1

    def kept(flag):
        return jnp.where(flag, 1.0, 0.0).astype(jnp.float32)

    for i in range(4):
        for t in range(4):
            xp, yp, zp = weight[0, i, t], weight[1, i, t], weight[2, i, t]
            xm = weight[0, i - 1, t] if i > 0 else edge_x[t] * kept(low_x)
            ym = jnp.where(
                row == 0, edge_y[4 * i + t : 4 * i + t + 1, :] * kept(low_y), pltpu.roll(yp, 1, axis=0)
            )
            if t > 0:
                zm = weight[2, i, t - 1]
            else:
                zm = jnp.where(
                    group == 0, roll_lanes(edge_z[i], 32) * kept(low_z), roll_lanes(weight[2, i, 3], 32)
                )
            coef[0, i, t] = ((xp + xm) + (yp + ym)) + (zp + zm) - CENTRE / WIDTH
            coef[1, i, t] = xp * kept(high_x) if i == 3 else xp
            coef[2, i, t] = xm
            coef[3, i, t] = jnp.where(row == 15, yp * kept(high_y), yp)
            coef[4, i, t] = ym
            coef[5, i, t] = jnp.where(group == 3, zp * kept(high_z), zp) if t == 3 else zp
            coef[6, i, t] = zm

    def apply_operator(level):
        for copy in rounds[level]:
            copy.wait_recv()
        for i in range(4):
            for t in range(4):
                centre = field[level, i, t]
                xp = field[level, i + 1, t] if i < 3 else halo_x[level, 1, t]
                xm = field[level, i - 1, t] if i > 0 else halo_x[level, 0, t]
                r = 4 * i + t
                yp = jnp.where(row == 15, halo_y[level, 1, r : r + 1, :], pltpu.roll(centre, 15, axis=0))
                ym = jnp.where(row == 0, halo_y[level, 0, r : r + 1, :], pltpu.roll(centre, 1, axis=0))
                if t < 3:
                    zp = field[level, i, t + 1]
                else:
                    zp = roll_lanes(jnp.where(group == 0, halo_z[level, 1, i], field[level, i, 0]), 96)
                if t > 0:
                    zm = field[level, i, t - 1]
                else:
                    zm = roll_lanes(jnp.where(group == 3, halo_z[level, 0, i], field[level, i, 3]), 32)
                value = coef[0, i, t] * centre
                value = value - (coef[1, i, t] * xp + coef[2, i, t] * xm)
                value = value - (coef[3, i, t] * yp + coef[4, i, t] * ym)
                value = value - (coef[5, i, t] * zp + coef[6, i, t] * zm)
                if level > 0:
                    value = value - field[level - 1, i, t]
                put(level + 1, i, t, value)
        if level + 1 < POWERS:
            for copy in rounds[level + 1]:
                copy.start()

    def products(m):
        for i in range(4):
            for g in range(4):
                for t in range(4):
                    k = 4 * g + t
                    rows = slice(16 * i, 16 * i + 16)
                    y = jnp.where(
                        group == 0,
                        roll_lanes(field[m, i, t], -BLOCK * g),
                        jnp.where(group == 1, roll_lanes(field[m - 1, i, t], BLOCK * (1 - g)), y_ref[k, rows, :]),
                    )
                    y_ref[k, rows, :] = y
                    if m == 2:
                        xa_ref[k, rows, :] = y
                    if m == 4:
                        xb_ref[k, rows, :] = jnp.where(lane < 64, y, xb_ref[k, rows, :])
        y = y_ref[...].reshape(1024, LANES)
        return lax.dot_general(
            y if m == 1 else y[:, :BLOCK],
            y,
            (((0,), (0,)), ((), ())),
            precision=lax.Precision.HIGH,
            preferred_element_type=jnp.float32,
        )

    class Stream:
        def __init__(self, n, rows, refs):
            self.n, self.chunk = n, rows // nx
            self.local, self.part_x, self.part_z, self.part_y, self.total = (
                refs.at[pl.ds(8 * q, 8)] for q in range(5)
            )
            self.whole = refs.at[40]

        def copy(self, src, dst, phase, device):
            return pltpu.make_async_remote_copy(
                src_ref=src,
                dst_ref=dst,
                send_sem=sum_send.at[self.n, phase],
                recv_sem=sum_recv.at[self.n, phase],
                device_id=device,
                device_id_type=MESH,
            )

        def all_of(self, ref, phase):
            axis = ("gx", "gz", "gy", "gx")[phase]
            part = ref.at[pl.ds(1, size_of[axis] - 1)]
            return self.copy(part, part, phase, partner(axis, 1))

        def begin(self, values):
            for c in range(nx):
                self.local[c] = values[c * self.chunk : (c + 1) * self.chunk, :]
            for d in range(1, nx):
                self.copy(self.local.at[gx ^ d], self.part_x.at[d], 0, partner("gx", d)).start()
            self.part_x[0] = self.local[gx]

        def over_z(self):
            self.all_of(self.part_x, 0).wait_recv()
            self.part_z[0] = tree_sum([self.part_x[d] for d in range(nx)])
            for d in range(1, nz):
                self.copy(self.part_z.at[0], self.part_z.at[d], 1, partner("gz", d)).start()

        def over_y(self):
            self.all_of(self.part_z, 1).wait_recv()
            self.part_y[0] = tree_sum([self.part_z[d] for d in range(nz)])
            for d in range(1, ny):
                self.copy(self.part_y.at[0], self.part_y.at[d], 2, partner("gy", d)).start()

        def gather(self):
            self.all_of(self.part_y, 2).wait_recv()
            self.whole[...] = tree_sum([self.part_y[d] for d in range(ny)])
            for d in range(1, nx):
                self.copy(self.whole, self.total.at[gx], 3, partner("gx", d)).start()
            self.total[gx] = self.whole[...]

        def result(self):
            self.all_of(self.total, 3).wait_recv()
            for c in range(nx):
                gathered[c * self.chunk : (c + 1) * self.chunk, :] = self.total[c]
            return gathered[0 : nx * self.chunk, :] * (1.0 / (1024 * nx * ny * nz))

        def drain(self):
            for phase, ref in enumerate((self.part_x, self.part_z, self.part_y, self.total)):
                self.all_of(ref, phase).wait_send()

    a = Stream(0, LANES, stream_a)
    s2, s3, s4 = (Stream(n, BLOCK, ref) for n, ref in ((1, stream_2), (2, stream_3), (3, stream_4)))

    t, tau = scalars(shift_ref[0])
    done = dict(coef=[], inverse=[], back=[])
    known = {}
    eliminate = eliminate_in(rows_ref)

    def block(m, values, prior):
        out = level_algebra(m, values, known, done, prior, tau, eliminate)
        rows = slice(BLOCK * (m - 1), BLOCK * m)
        maps_ref[rows, :] = out["maps"]
        small_ref[0, rows, :] = out["factor"]
        small_ref[1, rows, :] = out["upper"]
        small_ref[2, rows, :] = out["twice"]

    apply_operator(0)
    a.begin(products(1))
    apply_operator(1)
    a.over_z()
    s2.begin(products(2))
    apply_operator(2)
    a.over_y()
    s2.over_z()
    s3.begin(products(3))
    apply_operator(3)
    a.gather()
    s4.begin(products(4))
    s2.over_y()
    s3.over_z()
    s4.over_z()
    gram = a.result()
    known[0] = (gram[32:64, :], 1)
    prior = prior_algebra(gram, tau)
    small_ref[3] = prior["off2"]
    s2.gather()
    s3.over_y()
    block(1, gram[:BLOCK, :], prior)
    s4.over_y()
    s3.gather()
    block(2, s2.result(), prior)
    s4.gather()
    block(3, s3.result(), prior)
    block(4, s4.result(), prior)

    for copy in edges + [c for r in rounds for c in r]:
        copy.wait_send()
    for stream in (a, s2, s3, s4):
        stream.drain()


def basis_kernel(xa_ref, xb_ref, maps_ref, small_ref, shift_ref, new_ref, projection_ref, triangle_ref):
    maps = maps_ref[...]
    for k in range(16):
        both = jnp.concatenate([xa_ref[k], xb_ref[k]], axis=1)
        out = lax.dot_general(
            both,
            maps,
            (((1,), (1,)), ((), ())),
            precision=lax.Precision.HIGH,
            preferred_element_type=jnp.float32,
        )
        for i in range(4):
            new_ref[i, :, k * LANES : (k + 1) * LANES] = out[16 * i : 16 * i + 16, :]
    t, _ = scalars(shift_ref[0])
    projection, triangle = small_outputs(small_ref[0], small_ref[1], small_ref[2], small_ref[3], t)
    projection_ref[0:64, :] = projection[64:, :]
    projection_ref[64:96, :] = projection[32:64, :]
    triangle_ref[...] = triangle


def per_device(sizes, prior_basis, edge_weights, spectral_shift):
    nx, ny, nz = sizes
    f32 = jnp.float32
    tile = (4, 16, LANES)
    vmem = pl.BlockSpec(memory_space=pltpu.VMEM)
    smem = pl.BlockSpec(memory_space=pltpu.SMEM)
    hbm = pl.BlockSpec(memory_space=pltpu.HBM)
    xa, xb, maps, small = pl.pallas_call(
        functools.partial(powers_kernel, sizes),
        out_shape=(
            jax.ShapeDtypeStruct((16, 64, LANES), f32),
            jax.ShapeDtypeStruct((16, 64, LANES), f32),
            jax.ShapeDtypeStruct((LANES, 2 * LANES), f32),
            jax.ShapeDtypeStruct((4, LANES, LANES), f32),
        ),
        in_specs=[hbm, hbm, smem],
        out_specs=(vmem,) * 4,
        scratch_shapes=[
            pltpu.VMEM((4, 16, 16 * BASIS), f32),
            pltpu.VMEM((3, 4, 16, 16), f32),
            pltpu.VMEM((16, 64, LANES), f32),
            pltpu.VMEM((POWERS + 1, 4, *tile), f32),
            pltpu.VMEM((3, 4, *tile), f32),
            pltpu.VMEM((7, 4, *tile), f32),
            pltpu.VMEM((POWERS, 2, *tile), f32),
            pltpu.VMEM((POWERS, 2, 16, LANES), f32),
            pltpu.VMEM((POWERS, 2, *tile), f32),
            pltpu.VMEM((POWERS, 2, 16, LANES), f32),
            pltpu.VMEM(tile, f32),
            pltpu.VMEM((16, LANES), f32),
            pltpu.VMEM(tile, f32),
            pltpu.VMEM((16, LANES), f32),
            pltpu.VMEM((BLOCK, LANES), f32),
            pltpu.VMEM((LANES, LANES), f32),
            pltpu.VMEM((41, LANES // nx, LANES), f32),
            pltpu.VMEM((41, BLOCK // nx, LANES), f32),
            pltpu.VMEM((41, BLOCK // nx, LANES), f32),
            pltpu.VMEM((41, BLOCK // nx, LANES), f32),
            pltpu.SemaphoreType.DMA((2,)),
            pltpu.SemaphoreType.DMA((POWERS, 6)),
            pltpu.SemaphoreType.DMA((POWERS, 6)),
            pltpu.SemaphoreType.DMA((3,)),
            pltpu.SemaphoreType.DMA((3,)),
            pltpu.SemaphoreType.DMA((4, 4)),
            pltpu.SemaphoreType.DMA((4, 4)),
        ],
        name="powers",
        compiler_params=pltpu.CompilerParams(
            collective_id=0, has_side_effects=True, vmem_limit_bytes=40 * 2**20
        ),
    )(prior_basis, edge_weights, spectral_shift)
    return pl.pallas_call(
        basis_kernel,
        out_shape=(
            jax.ShapeDtypeStruct((4, 16, 16 * LANES), f32),
            jax.ShapeDtypeStruct((BASIS, LANES), f32),
            jax.ShapeDtypeStruct((LANES, LANES), f32),
        ),
        in_specs=[vmem, vmem, vmem, vmem, smem],
        out_specs=(vmem, vmem, vmem),
        name="basis",
        compiler_params=pltpu.CompilerParams(vmem_limit_bytes=32 * 2**20),
    )(xa, xb, maps, small, spectral_shift)


def solution(mesh):
    sizes = tuple(mesh.shape[a] for a in AXES)
    return jax.shard_map(
        functools.partial(per_device, sizes),
        mesh=mesh,
        in_specs=(P("gx", "gy", "gz"), P(None, "gx", "gy", "gz"), P()),
        out_specs=(P("gx", "gy", "gz"), P(), P()),
        check_vma=False,
    )
```

time: 67.2 us -> 62 us (0.923)
  Pallas kernels: 63.8 us -> 58.6 us
    pallas_call x1, Pallas kernels: 13.5 us -> 2.02 us  [per_device(): pl.pallas_call(basis_kernel, out_shape=(jax.ShapeDtypeStruct((4, 16, 16 *...]
    pallas_call x1, Pallas kernels: 50.3 us -> 56.6 us  [per_device(): pl.pallas_call(functools.partial(powers_kernel, sizes), out_shape=(jax.Sh...]
where the time goes in v2:
time: 62 us; the launch traced here: 61.8 us
  Pallas kernels  58.6 us (95%)
  local copies, waits for them, and re-layouts  1.88 us (3%)
  between operations  1.29 us (2%)
    pallas_call x1, Pallas kernels, per_device(): pl.pallas_call(functools.partial(powers_kernel, sizes), out_shape=(jax.Sh...  56.6 us
    pallas_call x1, Pallas kernels, per_device(): pl.pallas_call(basis_kernel, out_shape=(jax.ShapeDtypeStruct((4, 16, 16 *...  2.02 us
    unnamed x4, local copies, waits for them, and re-layouts  1.88 us

profile of v2, /device:TPU:1, one launch (start us, length us, event | category | flops | bytes accessed | tf_op | source)
XLA Modules:
  0.0 61.8 jit_solution(9580394361522647076)
XLA Ops:
  1.3 0.0 copy-start
  1.3 1.0 %copy-done = f32[4,16,1536]{2,1,0:T(8,128)S(1)} copy-done((f32[4,16,1536]{2,1,0:T(8,128)S(1)}, f32[4,16,1536]{2,1,0:T(8,128)}, u32[]{:S(2)}) %copy-start) | copy-done | bytes 393240
  2.3 0.0 copy-start.1
  2.3 0.9 %copy-done.1 = f32[3,4,16,16]{3,2,1,0:T(8,128)S(1)} copy-done((f32[3,4,16,16]{3,2,1,0:T(8,128)S(1)}, f32[3,4,16,16]{3,2,1,0:T(8,128)}, u32[]{:S(2)}) %copy-start.1) | copy-done | bytes 12312
  3.2 56.6 %powers.1 = (f32[16,64,128]{2,1,0:T(8,128)S(1)}, f32[16,64,128]{2,1,0:T(8,128)S(1)}, f32[128,256]{1,0:T(8,128)S(1)}, f32[4,128,128]{2,1,0:T(8,128)S(1)}) custom-call(f32[4,16,1536]{2,1,0:T(8,128)S(1)} %copy-done, f32[3,4,16,16]{3,2,1,0:T(8,128)S(1)} %copy-done.1, f32[1]{0:T(128)S(6)} %copy.6.shift_ref), custom_call_target="tpu_custom_call" | custom-call | tf_op jit(solution)/shard_map/powers/pallas_call | solution.py:604
  59.7 2.0 %basis.1 = (f32[4,16,2048]{2,1,0:T(8,128)}, f32[96,128]{1,0:T(8,128)}, f32[128,128]{1,0:T(8,128)}) custom-call(f32[16,64,128]{2,1,0:T(8,128)S(1)} %get-tuple-element.7.xa_ref, f32[16,64,128]{2,1,0:T(8,128)S(1)} %get-tuple-element.8.xb_ref, f32[128,256]{1,0:T(8,128)S(1)} %get-tuple-element.9.maps_ref, f32[4,128,128]{2,1,0:T(8,128)S(1)} %get-tuple-element.10.small_ref, ...), custom_call_target="tpu_custom_call" | custom-call | tf_op jit(solution)/shard_map/basis/pallas_call | solution.py:648
Async XLA Ops:
  1.3 1.0 %copy-start = (f32[4,16,1536]{2,1,0:T(8,128)S(1)}, f32[4,16,1536]{2,1,0:T(8,128)}, u32[]{:S(2)}) copy-start(f32[4,16,1536]{2,1,0:T(8,128)} %q_hbm.1) | copy-start | bytes 1179652
  2.3 0.9 %copy-start.1 = (f32[3,4,16,16]{3,2,1,0:T(8,128)S(1)}, f32[3,4,16,16]{3,2,1,0:T(8,128)}, u32[]{:S(2)}) copy-start(f32[3,4,16,16]{3,2,1,0:T(8,128)} %w_hbm.1) | copy-start | bytes 36868

commit v3 on v2

--- a/solution.py
+++ b/solution.py
@@ -201,19 +201,22 @@
     def run(work):
         sub = rows_of((8, LANES))
         a = [work[8 * b : 8 * b + 8, :] for b in range(4)]
-        for j in range(BLOCK):
-            b0, s = divmod(j, 8)
-            row = a[b0][s : s + 1, :]
-            root = lax.rsqrt(row[:, j : j + 1])
-            row = row * root
-            rows_ref[j : j + 1, :] = row
-            for b in range(b0, 4):
-                if b == b0 and s == 7:
-                    continue
-                column = a[b][:, j : j + 1] * root
-                if b == b0:
-                    column = jnp.where(sub > s, column, 0.0)
-                a[b] = a[b] - column * row
+        for b0 in range(4):
+            columns = [
+                [jnp.broadcast_to(a[b][:, 8 * b0 + n : 8 * b0 + n + 1], (8, LANES)) for b in range(b0, 4)]
+                for n in range(8)
+            ]
+            for s in range(8):
+                root = lax.rsqrt(columns[s][0][s : s + 1, :])
+                row = a[b0][s : s + 1, :] * root
+                rows_ref[8 * b0 + s : 8 * b0 + s + 1, :] = row
+                scaled = [c * root for c in columns[s]]
+                scaled[0] = jnp.where(sub > s, scaled[0], 0.0)
+                for n in range(s + 1, 8):
+                    weight = columns[n][0][s : s + 1, :] * root
+                    columns[n] = [c - m * weight for c, m in zip(columns[n], scaled)]
+                for b in range(b0, 4):
+                    a[b] = a[b] - scaled[b - b0] * row
         return rows_ref[...]
 
     return run
@@ -234,6 +237,9 @@
     field,
     weight,
     coef,
+    rim_x,
+    rim_y,
+    rim_z,
     halo_x,
     halo_y,
     halo_z,
@@ -280,10 +286,11 @@
 
     barrier = pltpu.get_barrier_semaphore()
     peers = 0
-    for axis in AXES:
-        for d in range(1, size_of[axis]):
-            pl.semaphore_signal(barrier, inc=1, device_id=partner(axis, d), device_id_type=MESH)
-            peers += 1
+    for d in range(max(sizes) - 1, 0, -1):
+        for axis in ("gy", "gz", "gx"):
+            if d < size_of[axis]:
+                pl.semaphore_signal(barrier, inc=1, device_id=partner(axis, d), device_id_type=MESH)
+                peers += 1
 
     lane = lax.broadcasted_iota(jnp.int32, (16, LANES), 1)
     row = lax.broadcasted_iota(jnp.int32, (16, LANES), 0)
@@ -390,71 +397,98 @@
 
     for i in range(4):
         for t in range(4):
+            r = slice(4 * i + t, 4 * i + t + 1)
             xp, yp, zp = weight[0, i, t], weight[1, i, t], weight[2, i, t]
-            xm = weight[0, i - 1, t] if i > 0 else edge_x[t] * kept(low_x)
-            ym = jnp.where(
-                row == 0, edge_y[4 * i + t : 4 * i + t + 1, :] * kept(low_y), pltpu.roll(yp, 1, axis=0)
-            )
+            if i > 0:
+                xm = weight[0, i - 1, t]
+            else:
+                xm = edge_x[t] * kept(low_x)
+                rim_x[0, t] = xm
+            if i == 3:
+                rim_x[1, t] = xp * kept(high_x)
+            below = edge_y[r, :] * kept(low_y)
+            rim_y[0, r, :] = below
+            rim_y[1, r, :] = yp[15:16, :] * kept(high_y)
+            ym = pltpu.roll(yp, 1, axis=0)
+            ym_all = jnp.where(row == 0, below, ym)
             if t > 0:
-                zm = weight[2, i, t - 1]
+                zm = zm_all = weight[2, i, t - 1]
             else:
-                zm = jnp.where(
-                    group == 0, roll_lanes(edge_z[i], 32) * kept(low_z), roll_lanes(weight[2, i, 3], 32)
-                )
-            coef[0, i, t] = ((xp + xm) + (yp + ym)) + (zp + zm) - CENTRE / WIDTH
-            coef[1, i, t] = xp * kept(high_x) if i == 3 else xp
+                rim = jnp.where(group == 0, roll_lanes(edge_z[i], 32) * kept(low_z), 0.0)
+                rim_z[0, i] = rim
+                zm = jnp.where(group == 0, 0.0, roll_lanes(weight[2, i, 3], 32))
+                zm_all = zm + rim
+            if t == 3:
+                rim_z[1, i] = jnp.where(group == 3, zp * kept(high_z), 0.0)
+            coef[0, i, t] = ((xp + xm) + (yp + ym_all)) + (zp + zm_all) - CENTRE / WIDTH
+            coef[1, i, t] = xp
             coef[2, i, t] = xm
-            coef[3, i, t] = jnp.where(row == 15, yp * kept(high_y), yp)
-            coef[4, i, t] = ym
-            coef[5, i, t] = jnp.where(group == 3, zp * kept(high_z), zp) if t == 3 else zp
+            coef[3, i, t] = jnp.where(row == 15, 0.0, yp)
+            coef[4, i, t] = jnp.where(row == 0, 0.0, ym)
+            coef[5, i, t] = jnp.where(group == 3, 0.0, zp) if t == 3 else zp
             coef[6, i, t] = zm
 
-    def apply_operator(level):
-        for copy in rounds[level]:
-            copy.wait_recv()
+    def apply_inside(level):
         for i in range(4):
             for t in range(4):
                 centre = field[level, i, t]
-                xp = field[level, i + 1, t] if i < 3 else halo_x[level, 1, t]
-                xm = field[level, i - 1, t] if i > 0 else halo_x[level, 0, t]
-                r = 4 * i + t
-                yp = jnp.where(row == 15, halo_y[level, 1, r : r + 1, :], pltpu.roll(centre, 15, axis=0))
-                ym = jnp.where(row == 0, halo_y[level, 0, r : r + 1, :], pltpu.roll(centre, 1, axis=0))
-                if t < 3:
-                    zp = field[level, i, t + 1]
-                else:
-                    zp = roll_lanes(jnp.where(group == 0, halo_z[level, 1, i], field[level, i, 0]), 96)
-                if t > 0:
-                    zm = field[level, i, t - 1]
-                else:
-                    zm = roll_lanes(jnp.where(group == 3, halo_z[level, 0, i], field[level, i, 3]), 32)
+                yp, ym = pltpu.roll(centre, 15, axis=0), pltpu.roll(centre, 1, axis=0)
+                zp = field[level, i, t + 1] if t < 3 else roll_lanes(field[level, i, 0], 96)
+                zm = field[level, i, t - 1] if t > 0 else roll_lanes(field[level, i, 3], 32)
                 value = coef[0, i, t] * centre
-                value = value - (coef[1, i, t] * xp + coef[2, i, t] * xm)
+                if i < 3:
+                    value = value - coef[1, i, t] * field[level, i + 1, t]
+                if i > 0:
+                    value = value - coef[2, i, t] * field[level, i - 1, t]
                 value = value - (coef[3, i, t] * yp + coef[4, i, t] * ym)
                 value = value - (coef[5, i, t] * zp + coef[6, i, t] * zm)
                 if level > 0:
                     value = value - field[level - 1, i, t]
+                field[level + 1, i, t] = value
+
+    def apply_faces(level):
+        for copy in rounds[level]:
+            copy.wait_recv()
+        following = rounds[level + 1] if level + 1 < POWERS else []
+        low = rim_y[0] * halo_y[level, 0]
+        high = rim_y[1] * halo_y[level, 1]
+        for i in (3, 0, 1, 2):
+            for t in range(4):
+                r = slice(4 * i + t, 4 * i + t + 1)
+                value = field[level + 1, i, t]
+                if i == 3:
+                    value = value - rim_x[1, t] * halo_x[level, 1, t]
+                if i == 0:
+                    value = value - rim_x[0, t] * halo_x[level, 0, t]
+                value = value - jnp.where(row == 0, low[r, :], jnp.where(row == 15, high[r, :], 0.0))
+                if t == 3:
+                    value = value - rim_z[1, i] * roll_lanes(halo_z[level, 1, i], 96)
+                if t == 0:
+                    value = value - rim_z[0, i] * roll_lanes(halo_z[level, 0, i], 32)
                 put(level + 1, i, t, value)
-        if level + 1 < POWERS:
-            for copy in rounds[level + 1]:
-                copy.start()
-
-    def products(m):
+            if i == 0:
+                for copy in following[:2]:
+                    copy.start()
+        for copy in following[2:]:
+            copy.start()
+
+    def prepare(m):
         for i in range(4):
+            rows = slice(16 * i, 16 * i + 16)
             for g in range(4):
                 for t in range(4):
                     k = 4 * g + t
-                    rows = slice(16 * i, 16 * i + 16)
-                    y = jnp.where(
-                        group == 0,
-                        roll_lanes(field[m, i, t], -BLOCK * g),
-                        jnp.where(group == 1, roll_lanes(field[m - 1, i, t], BLOCK * (1 - g)), y_ref[k, rows, :]),
+                    y_ref[k, rows, :] = jnp.where(
+                        group == 1, roll_lanes(field[m - 1, i, t], BLOCK * (1 - g)), y_ref[k, rows, :]
                     )
-                    y_ref[k, rows, :] = y
-                    if m == 2:
-                        xa_ref[k, rows, :] = y
-                    if m == 4:
-                        xb_ref[k, rows, :] = jnp.where(lane < 64, y, xb_ref[k, rows, :])
+
+    def products(m):
+        for i in range(4):
+            rows = slice(16 * i, 16 * i + 16)
+            for g in range(4):
+                for t in range(4):
+                    k = 4 * g + t
+                    y_ref[k, rows, :] = jnp.where(group == 0, roll_lanes(field[m, i, t], -BLOCK * g), y_ref[k, rows, :])
         y = y_ref[...].reshape(1024, LANES)
         return lax.dot_general(
             y if m == 1 else y[:, :BLOCK],
@@ -539,20 +573,32 @@
         small_ref[1, rows, :] = out["upper"]
         small_ref[2, rows, :] = out["twice"]
 
-    apply_operator(0)
+    apply_inside(0)
+    prepare(1)
+    apply_faces(0)
+    apply_inside(1)
     a.begin(products(1))
-    apply_operator(1)
+    prepare(2)
+    apply_faces(1)
+    apply_inside(2)
     a.over_z()
     s2.begin(products(2))
-    apply_operator(2)
+    xa_ref[...] = y_ref[...]
+    prepare(3)
+    apply_faces(2)
+    apply_inside(3)
     a.over_y()
     s2.over_z()
     s3.begin(products(3))
-    apply_operator(3)
+    prepare(4)
+    apply_faces(3)
+    s4.begin(products(4))
     a.gather()
-    s4.begin(products(4))
     s2.over_y()
     s3.over_z()
+    for k in range(16):
+        wide_lane = lax.broadcasted_iota(jnp.int32, (64, LANES), 1)
+        xb_ref[k] = jnp.where(wide_lane < 64, y_ref[k], xb_ref[k])
     s4.over_z()
     gram = a.result()
     known[0] = (gram[32:64, :], 1)
@@ -618,6 +664,9 @@
             pltpu.VMEM((POWERS + 1, 4, *tile), f32),
             pltpu.VMEM((3, 4, *tile), f32),
             pltpu.VMEM((7, 4, *tile), f32),
+            pltpu.VMEM((2, *tile), f32),
+            pltpu.VMEM((2, 16, LANES), f32),
+            pltpu.VMEM((2, *tile), f32),
             pltpu.VMEM((POWERS, 2, *tile), f32),
             pltpu.VMEM((POWERS, 2, 16, LANES), f32),
             pltpu.VMEM((POWERS, 2, *tile), f32),
@@ -644,7 +693,11 @@
         compiler_params=pltpu.CompilerParams(
             collective_id=0, has_side_effects=True, vmem_limit_bytes=40 * 2**20
         ),
-    )(prior_basis, edge_weights, spectral_shift)
+    )(
+        pltpu.with_memory_space_constraint(prior_basis, pltpu.HBM),
+        pltpu.with_memory_space_constraint(edge_weights, pltpu.HBM),
+        spectral_shift,
+    )
     return pl.pallas_call(
         basis_kernel,
         out_shape=(

time: 62 us -> 55.1 us (0.89)
  Pallas kernels: 58.6 us -> 53.6 us
  local copies, waits for them, and re-layouts: 1.88 us -> 0 us
    pallas_call x1, Pallas kernels: 56.6 us -> 51.6 us  [per_device(): pl.pallas_call(functools.partial(powers_kernel, sizes), out_shape=(jax.Sh...]
    unnamed x4 -> x0, local copies, waits for them, and re-layouts: 1.88 us -> none
where the time goes in v3:
time: 55.1 us; the launch traced here: 54.9 us
  Pallas kernels  53.6 us (97%)
  between operations  1.29 us (2%)
    pallas_call x1, Pallas kernels, per_device(): pl.pallas_call(functools.partial(powers_kernel, sizes), out_shape=(jax.Sh...  51.6 us
    pallas_call x1, Pallas kernels, per_device(): pl.pallas_call(basis_kernel, out_shape=(jax.ShapeDtypeStruct((4, 16, 16 *...  2.02 us

profile of v3, /device:TPU:1, one launch (start us, length us, event | category | flops | bytes accessed | tf_op | source)
XLA Modules:
  0.0 54.9 jit_solution(817604836882639835)
XLA Ops:
  1.3 51.6 %powers.1 = (f32[16,64,128]{2,1,0:T(8,128)S(1)}, f32[16,64,128]{2,1,0:T(8,128)S(1)}, f32[128,256]{1,0:T(8,128)S(1)}, f32[4,128,128]{2,1,0:T(8,128)S(1)}) custom-call(f32[4,16,1536]{2,1,0:T(8,128)} %q_hbm.1, f32[3,4,16,16]{3,2,1,0:T(8,128)} %w_hbm.1, f32[1]{0:T(128)S(6)} %copy.6.shift_ref), custom_call_target="tpu_custom_call" | custom-call | tf_op jit(solution)/shard_map/powers/pallas_call | solution.py:650
  52.9 2.0 %basis.1 = (f32[4,16,2048]{2,1,0:T(8,128)}, f32[96,128]{1,0:T(8,128)}, f32[128,128]{1,0:T(8,128)}) custom-call(f32[16,64,128]{2,1,0:T(8,128)S(1)} %get-tuple-element.7.xa_ref, f32[16,64,128]{2,1,0:T(8,128)S(1)} %get-tuple-element.8.xb_ref, f32[128,256]{1,0:T(8,128)S(1)} %get-tuple-element.9.maps_ref, f32[4,128,128]{2,1,0:T(8,128)S(1)} %get-tuple-element.10.small_ref, ...), custom_call_target="tpu_custom_call" | custom-call | tf_op jit(solution)/shard_map/basis/pallas_call | solution.py:701

commit v4 on v3

--- a/solution.py
+++ b/solution.py
@@ -244,6 +244,7 @@
     halo_y,
     halo_z,
     face_y,
+    face_z,
     edge_x,
     edge_y,
     edge_z,
@@ -261,6 +262,7 @@
     edge_recv,
     sum_send,
     sum_recv,
+    ready_sem,
 ):
     nx, ny, nz = sizes
     at = dict(zip(AXES, (lax.axis_index(a) for a in AXES)))
@@ -285,12 +287,9 @@
         copy.start()
 
     barrier = pltpu.get_barrier_semaphore()
-    peers = 0
-    for d in range(max(sizes) - 1, 0, -1):
-        for axis in ("gy", "gz", "gx"):
-            if d < size_of[axis]:
-                pl.semaphore_signal(barrier, inc=1, device_id=partner(axis, d), device_id_type=MESH)
-                peers += 1
+    for axis in AXES:
+        for step in (1, -1):
+            pl.semaphore_signal(barrier, inc=1, device_id=beside(axis, step), device_id_type=MESH)
 
     lane = lax.broadcasted_iota(jnp.int32, (16, LANES), 1)
     row = lax.broadcasted_iota(jnp.int32, (16, LANES), 0)
@@ -315,6 +314,12 @@
                 t,
                 pick([roll_lanes(q_tile(i, 3 * g + V_TILE[t]), BLOCK * g - V_LANE[t]) for g in range(4)]),
             )
+
+    def put_z(level):
+        face_z[level, 0] = pick([roll_lanes(field[level, i, 3], BLOCK * (i - 3)) for i in range(4)])
+        face_z[level, 1] = pick([roll_lanes(field[level, i, 0], BLOCK * i) for i in range(4)])
+
+    put_z(0)
 
     spread_k = lax.broadcasted_iota(jnp.int32, (16, 4 * LANES), 0)
     spread_lane = lax.broadcasted_iota(jnp.int32, (16, 4 * LANES), 1)
@@ -331,7 +336,7 @@
                 if d == 1:
                     face_wy[4 * i + t : 4 * i + t + 1, :] = value[15:16, :]
 
-    pl.semaphore_wait(barrier, peers)
+    pl.semaphore_wait(barrier, 6)
 
     def halo_copies(level):
         def copy(src, dst, n, device):
@@ -347,8 +352,8 @@
         return [
             copy(field.at[level, 3], halo_x.at[level, 0], 0, beside("gx", 1)),
             copy(field.at[level, 0], halo_x.at[level, 1], 1, beside("gx", -1)),
-            copy(field.at[level, :, 3], halo_z.at[level, 0], 2, beside("gz", 1)),
-            copy(field.at[level, :, 0], halo_z.at[level, 1], 3, beside("gz", -1)),
+            copy(face_z.at[level, 0], halo_z.at[level, 0], 2, beside("gz", 1)),
+            copy(face_z.at[level, 1], halo_z.at[level, 1], 3, beside("gz", -1)),
             copy(face_y.at[level, 0], halo_y.at[level, 0], 4, beside("gy", 1)),
             copy(face_y.at[level, 1], halo_y.at[level, 1], 5, beside("gy", -1)),
         ]
@@ -462,13 +467,15 @@
                     value = value - rim_x[0, t] * halo_x[level, 0, t]
                 value = value - jnp.where(row == 0, low[r, :], jnp.where(row == 15, high[r, :], 0.0))
                 if t == 3:
-                    value = value - rim_z[1, i] * roll_lanes(halo_z[level, 1, i], 96)
+                    value = value - rim_z[1, i] * roll_lanes(halo_z[level, 1], BLOCK * (3 - i))
                 if t == 0:
-                    value = value - rim_z[0, i] * roll_lanes(halo_z[level, 0, i], 32)
+                    value = value - rim_z[0, i] * roll_lanes(halo_z[level, 0], -BLOCK * i)
                 put(level + 1, i, t, value)
             if i == 0:
                 for copy in following[:2]:
                     copy.start()
+        if following:
+            put_z(level + 1)
         for copy in following[2:]:
             copy.start()
 
@@ -576,9 +583,14 @@
     apply_inside(0)
     prepare(1)
     apply_faces(0)
+    for axis in AXES:
+        for step in (2, -2):
+            pl.semaphore_signal(ready_sem, inc=1, device_id=beside(axis, step), device_id_type=MESH)
     apply_inside(1)
-    a.begin(products(1))
+    first = products(1)
     prepare(2)
+    pl.semaphore_wait(ready_sem, 6)
+    a.begin(first)
     apply_faces(1)
     apply_inside(2)
     a.over_z()
@@ -669,7 +681,8 @@
             pltpu.VMEM((2, *tile), f32),
             pltpu.VMEM((POWERS, 2, *tile), f32),
             pltpu.VMEM((POWERS, 2, 16, LANES), f32),
-            pltpu.VMEM((POWERS, 2, *tile), f32),
+            pltpu.VMEM((POWERS, 2, 16, LANES), f32),
+            pltpu.VMEM((POWERS, 2, 16, LANES), f32),
             pltpu.VMEM((POWERS, 2, 16, LANES), f32),
             pltpu.VMEM(tile, f32),
             pltpu.VMEM((16, LANES), f32),
@@ -688,6 +701,7 @@
             pltpu.SemaphoreType.DMA((3,)),
             pltpu.SemaphoreType.DMA((4, 4)),
             pltpu.SemaphoreType.DMA((4, 4)),
+            pltpu.SemaphoreType.REGULAR,
         ],
         name="powers",
         compiler_params=pltpu.CompilerParams(

time: 55.1 us -> 55.7 us (1.011)
  Pallas kernels: 53.6 us -> 54.3 us
    pallas_call x1, Pallas kernels: 51.6 us -> 52.3 us  [per_device(): pl.pallas_call(functools.partial(powers_kernel, sizes), out_shape=(jax.Sh...]
where the time goes in v4:
time: 55.7 us; the launch traced here: 55.6 us
  Pallas kernels  54.3 us (97%)
  between operations  1.29 us (2%)
    pallas_call x1, Pallas kernels, per_device(): pl.pallas_call(functools.partial(powers_kernel, sizes), out_shape=(jax.Sh...  52.3 us
    pallas_call x1, Pallas kernels, per_device(): pl.pallas_call(basis_kernel, out_shape=(jax.ShapeDtypeStruct((4, 16, 16 *...  2.02 us

profile of v4, /device:TPU:1, one launch (start us, length us, event | category | flops | bytes accessed | tf_op | source)
XLA Modules:
  0.0 55.6 jit_solution(9924935211017120745)
XLA Ops:
  1.3 52.3 %powers.1 = (f32[16,64,128]{2,1,0:T(8,128)S(1)}, f32[16,64,128]{2,1,0:T(8,128)S(1)}, f32[128,256]{1,0:T(8,128)S(1)}, f32[4,128,128]{2,1,0:T(8,128)S(1)}) custom-call(f32[4,16,1536]{2,1,0:T(8,128)} %q_hbm.1, f32[3,4,16,16]{3,2,1,0:T(8,128)} %w_hbm.1, f32[1]{0:T(128)S(6)} %copy.6.shift_ref), custom_call_target="tpu_custom_call" | custom-call | tf_op jit(solution)/shard_map/powers/pallas_call | solution.py:662
  53.6 2.0 %basis.1 = (f32[4,16,2048]{2,1,0:T(8,128)}, f32[96,128]{1,0:T(8,128)}, f32[128,128]{1,0:T(8,128)}) custom-call(f32[16,64,128]{2,1,0:T(8,128)S(1)} %get-tuple-element.7.xa_ref, f32[16,64,128]{2,1,0:T(8,128)S(1)} %get-tuple-element.8.xb_ref, f32[128,256]{1,0:T(8,128)S(1)} %get-tuple-element.9.maps_ref, f32[4,128,128]{2,1,0:T(8,128)S(1)} %get-tuple-element.10.small_ref, ...), custom_call_target="tpu_custom_call" | custom-call | tf_op jit(solution)/shard_map/basis/pallas_call | solution.py:715
